TPU v7x, 512 devices: a whole 4x8x8 slice. The times are simulated.
512 devices in a mesh: ctx: 64 (over y, z_lo, core), hid: 8 (over x, z_hi).
Axes of the slice: x: 4, y: 8, z: 8 (z_hi: 2, z_lo: 4; z = z_hi * 4 + z_lo), core: 2. Of those that a mesh axis runs over, the one named last changes fastest.
Arguments:
- q_act: bfloat16 [8192, 8192], P('ctx', 'hid'), may hold values from -6 to 6
- k_act: bfloat16 [8192, 8192], P('ctx', 'hid'), may hold values from -6 to 6
- v_act: bfloat16 [8192, 8192], P('ctx', 'hid'), may hold values from -6 to 6
- filt: float32 [128, 8192], P(None, 'hid'), may hold values from -0.5 to 0.5
- gain: float32 [8192], P('hid'), may hold values from 0.1 to 1.9
- segments: int32 [8192], P('ctx'), may hold values from 0 to 31, as said below
- grad_out: bfloat16 [8192, 8192], P('ctx', 'hid'), may hold values from -6 to 6
Outputs:
- layer_out: bfloat16 [8192, 8192], P('ctx', 'hid')
- q_grad: bfloat16 [8192, 8192], P('ctx', 'hid')
- k_grad: bfloat16 [8192, 8192], P('ctx', 'hid')
- v_grad: bfloat16 [8192, 8192], P('ctx', 'hid')
- filt_grad: float32 [128, 8192], P(None, 'hid')
- gain_grad: float32 [8192], P('hid')
Inputs may be any that keep to these rules, and one draw needn't show every extreme that they name: `segments`: ids start at 0, never fall and rise by at most one from one position to the next; there are exactly 32 documents, each spanning at least 128 positions.
All inputs are finite; a program needn't handle non-finite values.
Results may differ from a plain program's by a relative error of at most 0.005.
Values may be sent and summed in bfloat16 or wider, within the bound.
No kernel may reach another device: no remote copies, remote signals or barrier semaphores. Data moves between devices by JAX's collectives and lax.ppermute only.
A program may use at most 64 MiB of HBM per device.

v0:
```python
import jax
import jax.numpy as jnp
from jax import lax
from jax.sharding import PartitionSpec as P

C = 8192


def shifted(value, axis, steps):
    count = lax.axis_size(axis)
    first, last = (max(0, -steps), min(count, count - steps))
    return lax.ppermute(value, axis, [(source, source + steps) for source in range(first, last)])


def depthwise(source, kernel):
    return lax.conv_general_dilated(
        source,
        kernel[:, None, :],
        (1,),
        "VALID",
        dimension_numbers=("NWC", "WIO", "NWC"),
        feature_group_count=kernel.shape[1],
        precision=lax.Precision.HIGHEST,
    )


def split_planes(values, parity):
    return jnp.stack([values * (1.0 - parity)[:, None], values * parity[:, None]])


def pick_plane(both, parity):
    return both[0] * (1.0 - parity)[:, None] + both[1] * parity[:, None]


def correlate(dconv, parity, prod_pad, parity_pad):
    left_side = split_planes(dconv.astype(jnp.float32), parity)
    right_side = split_planes(prod_pad, parity_pad)
    source = jnp.concatenate([right_side[0], right_side[1]], axis=1)[None]
    kernel = jnp.concatenate([left_side[0], left_side[1]], axis=1)
    result = depthwise(source, kernel)[0]
    half = dconv.shape[1]
    return (result[:, :half] + result[:, half:])[::-1]


def local(q_act, k_act, v_act, filt, gain, segments, grad_out):
    rows_here = q_act.shape[0]
    width_here = q_act.shape[1]
    reach = filt.shape[0] - 1
    parity = (segments % 2).astype(jnp.float32)
    parity_half = parity.astype(jnp.bfloat16)
    prod = (k_act.astype(jnp.float32) * v_act.astype(jnp.float32)).astype(jnp.bfloat16)
    left_prod, left_parity = shifted(
        (prod[rows_here - reach :], parity_half[rows_here - reach :]), "ctx", 1
    )
    left_parity = left_parity.astype(jnp.float32)
    prod_pad = jnp.concatenate([left_prod, prod]).astype(jnp.float32)
    parity_pad = jnp.concatenate([left_parity, parity])
    conv = pick_plane(depthwise(split_planes(prod_pad, parity_pad), filt[::-1]), parity)
    query = q_act.astype(jnp.float32)
    y = query * conv
    upstream = grad_out.astype(jnp.float32)
    scaled_up = upstream * gain
    squares = lax.psum(jnp.sum(y * y, axis=1), "hid")
    rinv = lax.rsqrt(squares / C + 1e-06)
    inner = lax.psum(jnp.sum(scaled_up * y, axis=1), "hid")
    layer_out = (y * rinv[:, None] * gain).astype(jnp.bfloat16)
    gain_local = jnp.sum(upstream * y * rinv[:, None], axis=0)
    dy = rinv[:, None] * scaled_up - y * (rinv**3 * inner / C)[:, None]
    q_grad = (dy * conv).astype(jnp.bfloat16)
    dconv = (dy * query).astype(jnp.bfloat16)
    dconv_pad = jnp.concatenate([dconv, jnp.zeros((reach, width_here), jnp.bfloat16)]).astype(
        jnp.float32
    )
    parity_next = jnp.concatenate([parity, jnp.zeros((reach,), jnp.float32)])
    dprod_own = pick_plane(depthwise(split_planes(dconv_pad, parity_next), filt), parity)
    head_rows = jnp.concatenate(
        [jnp.zeros((reach, width_here), jnp.float32), dconv[:reach].astype(jnp.float32)]
    )
    head_parity = jnp.concatenate([jnp.zeros((reach,), jnp.float32), parity[:reach]])
    outgoing = pick_plane(depthwise(split_planes(head_rows, head_parity), filt), left_parity)
    incoming = shifted(outgoing, "ctx", -1)
    dprod = dprod_own + jnp.concatenate(
        [jnp.zeros((rows_here - reach, width_here), jnp.float32), incoming]
    )
    k_grad = (dprod * v_act.astype(jnp.float32)).astype(jnp.bfloat16)
    v_grad = (dprod * k_act.astype(jnp.float32)).astype(jnp.bfloat16)
    filt_local = correlate(dconv, parity, prod_pad, parity_pad)
    filt_grad, gain_grad = lax.psum((filt_local, gain_local), "ctx")
    return (layer_out, q_grad, k_grad, v_grad, filt_grad, gain_grad)


def solution(mesh):
    in_specs = (
        P("ctx", "hid"),
        P("ctx", "hid"),
        P("ctx", "hid"),
        P(None, "hid"),
        P("hid"),
        P("ctx"),
        P("ctx", "hid"),
    )
    out_specs = (
        P("ctx", "hid"),
        P("ctx", "hid"),
        P("ctx", "hid"),
        P("ctx", "hid"),
        P(None, "hid"),
        P("hid"),
    )
    return jax.shard_map(local, mesh=mesh, in_specs=in_specs, out_specs=out_specs, check_vma=False)
```

profile of v0, /device:TPU:1, one launch (start us, length us, event | category | flops | bytes accessed | tf_op | source)
XLA Modules:
  0.0 687.6 jit_solution(2085392831456655286)
XLA Ops:
  7.2 0.0 copy-start.4
  7.2 0.0 all-reduce.7.cloned.1.call-start
  7.2 0.7 broadcast_subtract_fusion.4
  7.9 0.1 slice.37
  8.0 5.4 collective-permute-start.1
  13.4 1.1 fusion.21
  14.5 0.1 slice.48
  14.6 1.9 collective-permute-start
  16.5 0.1 broadcast_subtract_fusion
  16.6 0.4 copy.42
  17.0 0.0 copy-done.4
  17.0 0.2 rev.6
  17.3 0.0 collective-permute-done.1
  17.3 0.1 broadcast_subtract_fusion.1
  17.4 2.4 collective-permute-done
  19.8 0.4 copy.41
  20.2 3.3 broadcast_multiply_fusion.1
  23.5 11.3 %fusion = f32[2,128,1024]{2,0,1:T(2,128)S(1)} fusion(f32[1,255,1024]{2,0,1:T(1,128)S(1)} %get-tuple-element.22, f32[1,255,1024]{2,0,1:T(1,128)S(1)} %get-tuple-element.21, f32[128,1,1024]{2,0,1:T(8,128)S(1)} %bitcast.67), kind=kOutput, calls=%fused_computation.3 | convolution fusion | flops 403175424 | bytes 3661824 | tf_op jit(solution)/shard_map/conv_general_dilated | solution.py:16
  34.7 0.0 copy-start
  34.7 0.0 copy-start.1
  34.8 0.0 copy-start.5
  34.8 0.8 fusion.47
  35.6 0.1 copy-done
  35.7 0.4 multiply_reduce_fusion
  36.1 30.4 %psum.28 = f32[128]{0:T(128)S(1)} all-reduce(f32[128]{0:T(128)S(1)} %get-tuple-element.12), channel_id=1, replica_groups=mesh['ctx'=64,'hid'=8] {'hid'}, use_global_device_ids=true, to_apply=%region_1.2 | all-reduce | flops 128 | bytes 1024 | tf_op jit(solution)/shard_map/psum | solution.py:63
  66.5 0.0 copy-done.1
  66.5 0.0 copy-done.5
  66.5 0.2 fusion.24
  66.7 20.4 %psum.29 = f32[128]{0:T(128)S(1)} all-reduce(f32[128]{0:T(128)S(1)} %get-tuple-element.7), channel_id=1, replica_groups=mesh['ctx'=64,'hid'=8] {'hid'}, use_global_device_ids=true, to_apply=%region_3.4 | all-reduce | flops 128 | bytes 1024 | tf_op jit(solution)/shard_map/psum | solution.py:65
  87.1 1.1 convert_multiply_fusion.7
  88.2 0.2 fusion.12
  88.4 0.1 pad_maximum_fusion.1
  88.6 10.5 %fusion.8 = f32[2,127,1024]{2,0,1:T(2,128)S(1)} fusion(f32[2,254,1024]{2,1,0:T(8,128)S(1)} %pad_maximum_fusion.1, f32[128,1,1024]{2,0,1:T(8,128)S(1)} %bitcast.65), kind=kOutput, calls=%fused_computation.11 | convolution fusion | flops 399507456 | bytes 3645440 | tf_op jit(solution)/shard_map/conv_general_dilated | solution.py:16
  99.1 0.8 fusion.48
  99.9 0.2 fusion.26
  100.1 7.7 %collective-permute-start.2 = (f32[127,1024]{1,0:T(8,128)S(1)}, f32[127,1024]{1,0:T(8,128)S(1)}, u32[]{:S(2)}, u32[]{:S(2)}) collective-permute-start(f32[127,1024]{1,0:T(8,128)S(1)} %fusion.26), channel_id=1, source_target_pairs={{8,0},{16,8},{24,16},{32,24},{40,32},{48,40},{56,48},{64,56},{72,6... | collective-permute-start | bytes 1560584 | tf_op jit(solution)/shard_map/ppermute | solution.py:12
  107.8 0.2 fusion.10
  108.0 0.1 pad_maximum_fusion
  108.2 10.4 %fusion.6 = f32[2,128,1024]{2,0,1:T(2,128)S(1)} fusion(f32[2,255,1024]{2,1,0:T(8,128)S(1)} %pad_maximum_fusion, f32[128,1,1024]{2,0,1:T(8,128)S(1)} %bitcast.66), kind=kOutput, calls=%fused_computation.9 | convolution fusion | flops 402653184 | bytes 3661824 | tf_op jit(solution)/shard_map/conv_general_dilated | solution.py:16
  118.6 0.2 convert_multiply_fusion.1
  118.9 0.8 fusion.46
  119.7 0.0 copy-start.2
  119.7 0.2 maximum_bitcast_fusion
  119.9 0.0 collective-permute-done.2
  119.9 0.7 copy-done.2
  120.6 1.1 fusion.20
  121.7 0.1 maximum_bitcast_fusion.1
  121.8 11.7 %fusion.4 = f32[1,128,2048]{2,0,1:T(1,128)S(1)} fusion(f32[1,255,2048]{2,1,0:T(8,128)S(1)} %maximum_bitcast_fusion, f32[128,1,2048]{2,0,1:T(8,128)S(1)} %maximum_bitcast_fusion.1), kind=kOutput, calls=%fused_computation.7 | convolution fusion | flops 402653184 | bytes 4186112 | tf_op jit(solution)/shard_map/conv_general_dilated | solution.py:16
  133.5 0.3 copy.110
  133.8 0.0 copy-start.3
  133.9 0.1 slice_add_fusion
  133.9 2.6 rev.7
  136.5 0.0 all-reduce.7.cloned.1.call-update
  136.6 137.2 %psum.31 = f32[1024]{0:T(1024)} all-reduce(f32[1024]{0:T(1024)S(1)} %get-tuple-element.6), channel_id=1, replica_groups=mesh['ctx'=64,'hid'=8] {'ctx'}, use_global_device_ids=true, to_apply=%region_6.7 | all-reduce | flops 1024 | bytes 8192 | tf_op jit(solution)/shard_map/psum | solution.py:88
  273.8 0.0 copy-done.3
  273.8 0.8 fusion.22
  274.5 404.3 %all-reduce.7.cloned.1.call-done = f32[128,1024]{1,0:T(8,128)} async-done(((f32[128,1024]{1,0:T(8,128)}), f32[128,1024]{1,0:T(8,128)}) %all-reduce.7.cloned.1.call-update) | async-done | bytes 524304 | tf_op jit(solution)/shard_map/psum | solution.py:88
  678.9 1.9 copy.112
  (5 shorter events, 0.0 us)
Async XLA Ops:
  7.2 9.8 %copy-start.4 = (f32[128,1024]{1,0:T(8,128)S(1)}, f32[128,1024]{1,0:T(8,128)}, u32[]{:S(2)}) copy-start(f32[128,1024]{1,0:T(8,128)} %param.10) | copy-start | bytes 1572868
  7.2 671.7 %all-reduce.7.cloned.1.call-start = ((), (), s32[]{:S(2)}) async-start(), calls=%async_computation | async-start | bytes 1048576 | tf_op jit(solution)/shard_map/psum | solution.py:88
  8.0 9.2 %collective-permute-start.1 = (bf16[127]{0:T(256)(128)(2,1)S(1)}, bf16[127]{0:T(256)(128)(2,1)S(1)}, u32[]{:S(2)}, u32[]{:S(2)}) collective-permute-start(bf16[127]{0:T(256)(128)(2,1)S(1)} %slice.37), channel_id=1, source_target_pairs={{0,8},{8,16},{16,24},{24,32},{32,40},{40,48},{48,56},{56,64},{64,7... | collective-permute-start | bytes 770 | tf_op jit(solution)/shard_map/ppermute | solution.py:12
  14.6 5.2 collective-permute-start
  34.7 1.0 copy-start
  34.7 31.8 %copy-start.1 = (bf16[128,1024]{1,0:T(8,128)(2,1)S(1)}, bf16[128,1024]{1,0:T(8,128)(2,1)}, u32[]{:S(2)}) copy-start(bf16[128,1024]{1,0:T(8,128)(2,1)} %param.13) | copy-start | bytes 786436
  34.8 31.8 %copy-start.5 = (f32[1024]{0:T(1024)S(1)}, f32[1024]{0:T(1024)}, u32[]{:S(2)}) copy-start(f32[1024]{0:T(1024)} %param.11) | copy-start | bytes 12292
  100.1 19.8 %collective-permute-start.2 = (f32[127,1024]{1,0:T(8,128)S(1)}, f32[127,1024]{1,0:T(8,128)S(1)}, u32[]{:S(2)}, u32[]{:S(2)}) collective-permute-start(f32[127,1024]{1,0:T(8,128)S(1)} %fusion.26), channel_id=1, source_target_pairs={{8,0},{16,8},{24,16},{32,24},{40,32},{48,40},{56,48},{64,56},{72,6... | collective-permute-start | bytes 1560584 | tf_op jit(solution)/shard_map/ppermute | solution.py:12
  119.7 1.0 copy-start.2
  133.8 139.9 %copy-start.3 = (bf16[128,1024]{1,0:T(8,128)(2,1)S(1)}, bf16[128,1024]{1,0:T(8,128)(2,1)}, u32[]{:S(2)}) copy-start(bf16[128,1024]{1,0:T(8,128)(2,1)} %param.9) | copy-start | bytes 786436
Sparse Core Ops, SparseCore 0:
  136.7 542.1 all-reduce.6
where the time goes:
time: 688 us
  waiting for transfers between devices  407 us (59%)
  blocking collectives  188 us (27%)
  matrix products  43.9 us (6%)
  starting transfers between devices  15 us (2%)
  between operations  14.3 us (2%)
  other arithmetic  10.3 us (1%)
  local copies, waits for them, and re-layouts  9.31 us (1%)
    psum x1, waiting for transfers between devices, local(): filt_grad, gain_grad = lax.psum((filt_local, gain_local), 'ctx')  404 us
    psum x1, blocking collectives, local(): filt_grad, gain_grad = lax.psum((filt_local, gain_local), 'ctx')  137 us
    conv_general_dilated x4, matrix products, depthwise(): lax.conv_general_dilated(source, kernel[:, None, :], (1,), 'VALID', dimen...  43.9 us
    psum x1, blocking collectives, local(): squares = lax.psum(jnp.sum(y * y, axis=1), 'hid')  30.4 us
    psum x1, blocking collectives, local(): inner = lax.psum(jnp.sum(scaled_up * y, axis=1), 'hid')  20.4 us
    ppermute x3, starting transfers between devices, shifted(): lax.ppermute(value, axis, [(source, source + steps) for source in range(f...  15 us
  transfers between devices with their start and end apart: 4, of which 2 were waited for; matrix products, arithmetic and copies ran while one was open for 2% of the time, Pallas kernels for 0%

commit v1 on v0

v1 whole, which is shorter than its diff:
```python
import jax
import jax.numpy as jnp
import ml_dtypes
import numpy as np
from jax import lax
from jax.experimental import pallas as pl
from jax.experimental.pallas import tpu as pltpu
from jax.sharding import PartitionSpec as P

C = 8192
ROWS = 128
FREQ = 128
BLOCK = 256


def split_const(matrix):
    high = matrix.astype(ml_dtypes.bfloat16)
    low = (matrix - high.astype(np.float64)).astype(ml_dtypes.bfloat16)
    return high, low


def transforms():
    omega = 2.0 * np.pi * (np.arange(FREQ) + 0.5) / (2 * FREQ)

    def at(positions):
        angle = omega[:, None] * positions[None, :]
        return np.concatenate([np.cos(angle), -np.sin(angle)], axis=0)

    here = np.arange(ROWS)
    own = at(here)
    left = at(here - ROWS)
    left[:, 0] = 0.0
    right = at(here + ROWS)
    right[:, -1] = 0.0
    own_hl = np.concatenate(split_const(own), axis=1)
    left_hl = np.concatenate(split_const(left), axis=1)
    right_hl = np.concatenate(split_const(right), axis=1)
    back_hl = np.concatenate(split_const(own.T / FREQ), axis=0)
    return own_hl, left_hl, right_hl, back_hl


def mm(a, b):
    return jnp.dot(a, b, preferred_element_type=jnp.float32)


def forward(matrix_hl, x):
    return mm(matrix_hl, jnp.concatenate([x, x], axis=0))


def forward_wide(matrix_hl, x):
    high = x.astype(jnp.bfloat16)
    low = (x - high.astype(jnp.float32)).astype(jnp.bfloat16)
    return forward(matrix_hl, high) + mm(matrix_hl[:, :ROWS], low)


def backward(back_hl, spectrum):
    high = spectrum.astype(jnp.bfloat16)
    low = (spectrum - high.astype(jnp.float32)).astype(jnp.bfloat16)
    both = mm(back_hl, high)
    return both[:ROWS] + both[ROWS:] + mm(back_hl[:ROWS], low)


def times(a, b):
    ar, ai, br, bi = a[:FREQ], a[FREQ:], b[:FREQ], b[FREQ:]
    return jnp.concatenate([ar * br - ai * bi, ar * bi + ai * br], axis=0)


def times_conj(a, b):
    ar, ai, br, bi = a[:FREQ], a[FREQ:], b[:FREQ], b[FREQ:]
    return jnp.concatenate([ar * br + ai * bi, ai * br - ar * bi], axis=0)


def down(row, width):
    square = jnp.broadcast_to(row, (ROWS, ROWS)).T
    return jnp.concatenate([square] * (width // ROWS), axis=1)


def first_doc(seg):
    return (seg == seg[:, :1]).astype(jnp.float32)


def last_doc(seg):
    return (seg == seg[:, ROWS - 1 :]).astype(jnp.float32)


def product(k_ref, v_ref):
    return (k_ref[...].astype(jnp.float32) * v_ref[...].astype(jnp.float32)).astype(jnp.bfloat16)


def conv_kernel(own_ref, left_ref, back_ref, seg_ref, k_ref, v_ref, halo_ref, filt_ref, q_ref, g_ref, gain_ref, conv_ref, stats_ref, sums):
    step = pl.program_id(0)
    width = k_ref.shape[1]
    seg = seg_ref[...]
    own, left, back = own_ref[...], left_ref[...], back_ref[...]
    in_first = down(first_doc(seg), width)
    prod = product(k_ref, v_ref)
    rest = prod * (1.0 - in_first).astype(jnp.bfloat16)
    parity = (seg[:, :1] % 2).astype(jnp.float32)
    joined = (halo_ref[0:1, :].astype(jnp.float32) == parity).astype(jnp.float32)
    taps = forward_wide(own, filt_ref[...])
    all_spec = forward(own, prod) + forward(left, halo_ref[...]) * joined
    rest_spec = forward(own, rest)
    conv_first = backward(back, times(all_spec, taps))
    conv_rest = backward(back, times(rest_spec, taps))
    conv = jnp.where(in_first > 0.5, conv_first, conv_rest)
    conv_ref[...] = conv
    y = q_ref[...].astype(jnp.float32) * conv
    gy = g_ref[...].astype(jnp.float32) * gain_ref[...]
    square, inner = y * y, gy * y
    square = sum(square[:, i * ROWS : (i + 1) * ROWS] for i in range(width // ROWS))
    inner = sum(inner[:, i * ROWS : (i + 1) * ROWS] for i in range(width // ROWS))

    @pl.when(step == 0)
    def _():
        sums[0] = square
        sums[1] = inner

    @pl.when(step > 0)
    def _():
        sums[0] += square
        sums[1] += inner

    @pl.when(step == pl.num_programs(0) - 1)
    def _():
        rows = jnp.concatenate(
            [jnp.sum(sums[0].T, axis=0, keepdims=True), jnp.sum(sums[1].T, axis=0, keepdims=True)], axis=0
        )
        stats_ref[...] = jnp.broadcast_to(rows[None], stats_ref.shape)


def scales(stats_ref):
    total = jnp.sum(stats_ref[...], axis=0)
    rinv = lax.rsqrt(total[0:1] / C + 1e-06)
    return rinv, rinv * rinv * rinv * total[1:2] / C


def grad_kernel(own_ref, left_ref, back_ref, seg_ref, k_ref, v_ref, halo_ref, q_ref, g_ref, gain_ref, conv_ref, stats_ref, chunk_ref, dconv_ref, head_ref):
    width = k_ref.shape[1]
    seg = seg_ref[...]
    own, left, back = own_ref[...], left_ref[...], back_ref[...]
    rinv, slope = scales(stats_ref)
    rinv, slope = down(rinv, width), down(slope, width)
    in_first = down(first_doc(seg), width)
    query = q_ref[...].astype(jnp.float32)
    up = g_ref[...].astype(jnp.float32)
    y = query * conv_ref[...]
    dy = rinv * (up * gain_ref[...]) - y * slope
    dconv = (dy * query).astype(jnp.bfloat16)
    dconv_ref[...] = dconv
    first_half = in_first.astype(jnp.bfloat16)
    d_first = dconv * first_half
    row = lax.broadcasted_iota(jnp.int32, (ROWS, width), 0)
    parity = (seg[:, :1] % 2).astype(jnp.float32)
    head_ref[...] = jnp.where(row == ROWS - 1, parity, d_first.astype(jnp.float32)).astype(jnp.bfloat16)
    d_rest = dconv - d_first
    prod = product(k_ref, v_ref)
    rest = prod * (1.0 - in_first).astype(jnp.bfloat16)
    joined = (halo_ref[0:1, :].astype(jnp.float32) == parity).astype(jnp.float32)
    all_spec = forward(own, prod) + forward(left, halo_ref[...]) * joined
    rest_spec = forward(own, rest)
    spectrum = times_conj(forward(own, d_first), all_spec) + times_conj(forward(own, d_rest), rest_spec)
    taps = backward(back, spectrum).astype(jnp.bfloat16)
    gain_sum = jnp.sum(up * y * rinv, axis=0, keepdims=True)
    gain_high = gain_sum.astype(jnp.bfloat16)
    gain_low = (gain_sum - gain_high.astype(jnp.float32)).astype(jnp.bfloat16)
    gain_both = jnp.concatenate([gain_high, gain_low], axis=0)
    for block in range(width // ROWS):
        lanes = slice(block * ROWS, (block + 1) * ROWS)
        for group in range(8):
            for pair in range(8):
                at = group * 16 + pair * 2
                chunk_ref[group, block, pair] = taps[at : at + 2, lanes]
            chunk_ref[group, block, 8] = gain_both[:, lanes]


def out_kernel(own_ref, right_ref, back_ref, seg_ref, k_ref, v_ref, q_ref, g_ref, gain_ref, conv_ref, stats_ref, dconv_ref, tail_ref, filt_ref, layer_ref, qg_ref, kg_ref, vg_ref):
    width = k_ref.shape[1]
    seg = seg_ref[...]
    own, right, back = own_ref[...], right_ref[...], back_ref[...]
    rinv, slope = scales(stats_ref)
    rinv, slope = down(rinv, width), down(slope, width)
    conv = conv_ref[...]
    y = q_ref[...].astype(jnp.float32) * conv
    gain = gain_ref[...]
    dy = rinv * (g_ref[...].astype(jnp.float32) * gain) - y * slope
    layer_ref[...] = (y * rinv * gain).astype(jnp.bfloat16)
    qg_ref[...] = (dy * conv).astype(jnp.bfloat16)
    dconv = dconv_ref[...]
    in_first = down(first_doc(seg), width)
    in_last = down(last_doc(seg), width)
    parity = (seg[:, ROWS - 1 :] % 2).astype(jnp.float32)
    joined = (tail_ref[ROWS - 1 :, :].astype(jnp.float32) == parity).astype(jnp.float32)
    taps = forward_wide(own, filt_ref[...])
    first_spec = forward(own, dconv * in_first.astype(jnp.bfloat16))
    all_spec = forward(own, dconv) + forward(right, tail_ref[...]) * joined
    dprod_last = backward(back, times_conj(all_spec, taps))
    dprod_first = backward(back, times_conj(first_spec, taps))
    dprod = jnp.where(in_last > 0.5, dprod_last, dprod_first)
    kg_ref[...] = (dprod * v_ref[...].astype(jnp.float32)).astype(jnp.bfloat16)
    vg_ref[...] = (dprod * k_ref[...].astype(jnp.float32)).astype(jnp.bfloat16)


def whole(shape):
    return pl.BlockSpec(shape, lambda i: (0,) * len(shape))


def columns(rows):
    return pl.BlockSpec((rows, BLOCK), lambda i: (0, i))


def params():
    return pltpu.CompilerParams(vmem_limit_bytes=48 * 1024 * 1024, dimension_semantics=("arbitrary",))


def cost(flops, moved):
    return pl.CostEstimate(flops=flops, bytes_accessed=moved, transcendentals=0)


def shifted(value, axis, steps):
    count = lax.axis_size(axis)
    first, last = (max(0, -steps), min(count, count - steps))
    return lax.ppermute(value, axis, [(source, source + steps) for source in range(first, last)])


def local(q_act, k_act, v_act, filt, gain, segments, grad_out):
    width = q_act.shape[1]
    n_ctx, n_hid = lax.axis_size("ctx"), lax.axis_size("hid")
    steps = width // BLOCK
    own_hl, left_hl, right_hl, back_hl = (jnp.asarray(m) for m in transforms())
    seg = segments.reshape(1, ROWS)
    gain_row = gain.reshape(1, width)
    act = jax.ShapeDtypeStruct((ROWS, width), jnp.bfloat16)

    prod = (k_act.astype(jnp.float32) * v_act.astype(jnp.float32)).astype(jnp.bfloat16)
    in_last = (segments == segments[ROWS - 1]).astype(jnp.bfloat16)
    row = lax.broadcasted_iota(jnp.int32, (ROWS, width), 0)
    message = jnp.where(row == 0, (segments[ROWS - 1] % 2).astype(jnp.bfloat16), prod * in_last[:, None])
    halo = shifted(message, "ctx", 1)

    wide, square = whole((256, 256)), whole((1, ROWS))
    stats_spec = whole((n_hid, 2, ROWS))
    conv, stats = pl.pallas_call(
        conv_kernel,
        grid=(steps,),
        in_specs=[wide, wide, wide, square, columns(ROWS), columns(ROWS), columns(ROWS), columns(ROWS), columns(ROWS), columns(ROWS), columns(1)],
        out_specs=[columns(ROWS), stats_spec],
        out_shape=[jax.ShapeDtypeStruct((ROWS, width), jnp.float32), jax.ShapeDtypeStruct((n_hid, 2, ROWS), jnp.float32)],
        scratch_shapes=[pltpu.VMEM((2, ROWS, ROWS), jnp.float32)],
        compiler_params=params(),
        cost_estimate=cost(8 * 2**27, 3 * 2**20),
        name="conv_stats",
    )(own_hl, left_hl, back_hl, seg, k_act, v_act, halo, filt, q_act, grad_out, gain_row)
    stats = lax.all_to_all(stats, "hid", 0, 0, tiled=True)

    groups = (8, width // ROWS, 9, 2, ROWS)
    chunks, dconv, head = pl.pallas_call(
        grad_kernel,
        grid=(steps,),
        in_specs=[wide, wide, wide, square, columns(ROWS), columns(ROWS), columns(ROWS), columns(ROWS), columns(ROWS), columns(1), columns(ROWS), stats_spec],
        out_specs=[pl.BlockSpec((8, BLOCK // ROWS, 9, 2, ROWS), lambda i: (0, i, 0, 0, 0)), columns(ROWS), columns(ROWS)],
        out_shape=[jax.ShapeDtypeStruct(groups, jnp.bfloat16), act, act],
        compiler_params=params(),
        cost_estimate=cost(8 * 2**27, 3 * 2**20),
        name="filter_grad",
    )(own_hl, left_hl, back_hl, seg, k_act, v_act, halo, q_act, grad_out, gain_row, conv, stats)

    chunks = chunks.reshape(n_ctx, 9, 2, ROWS)
    parts = lax.all_to_all(chunks, "ctx", 0, 0, tiled=True)
    tail = shifted(head, "ctx", -1)

    layer_out, q_grad, k_grad, v_grad = pl.pallas_call(
        out_kernel,
        grid=(steps,),
        in_specs=[wide, wide, wide, square, columns(ROWS), columns(ROWS), columns(ROWS), columns(ROWS), columns(1), columns(ROWS), stats_spec, columns(ROWS), columns(ROWS), columns(ROWS)],
        out_specs=[columns(ROWS)] * 4,
        out_shape=[act] * 4,
        compiler_params=params(),
        cost_estimate=cost(8 * 2**27, 4 * 2**20),
        name="input_grads",
    )(own_hl, right_hl, back_hl, seg, k_act, v_act, q_act, grad_out, gain_row, conv, stats, dconv, tail, filt)

    total = jnp.sum(parts.astype(jnp.float32), axis=0)
    gain_total = total[8, 0] + total[8, 1]
    gain_high = gain_total.astype(jnp.bfloat16)
    gain_low = (gain_total - gain_high.astype(jnp.float32)).astype(jnp.bfloat16)
    mine = jnp.concatenate([total[:8].astype(jnp.bfloat16), jnp.stack([gain_high, gain_low])[None]], axis=0)
    full = lax.all_to_all(jnp.broadcast_to(mine[None], parts.shape), "ctx", 0, 0, tiled=True)
    full = full.reshape(groups)
    filt_grad = full[:, :, :8].transpose(0, 2, 3, 1, 4).reshape(ROWS, width).astype(jnp.float32)
    gain_grad = (full[0, :, 8, 0].astype(jnp.float32) + full[0, :, 8, 1].astype(jnp.float32)).reshape(width)
    return (layer_out, q_grad, k_grad, v_grad, filt_grad, gain_grad)


def solution(mesh):
    in_specs = (
        P("ctx", "hid"),
        P("ctx", "hid"),
        P("ctx", "hid"),
        P(None, "hid"),
        P("hid"),
        P("ctx"),
        P("ctx", "hid"),
    )
    out_specs = (
        P("ctx", "hid"),
        P("ctx", "hid"),
        P("ctx", "hid"),
        P("ctx", "hid"),
        P(None, "hid"),
        P("hid"),
    )
    return jax.shard_map(local, mesh=mesh, in_specs=in_specs, out_specs=out_specs, check_vma=False)
```

time: 688 us -> 98.4 us (0.14)
  waiting for transfers between devices: 407 us -> 12.8 us
  blocking collectives: 188 us -> 47.2 us
  matrix products: 43.9 us -> 0 us
  between operations: 14.3 us -> 2.8 us
  Pallas kernels: 0 us -> 10.7 us
  other arithmetic: 10.3 us -> 2.84 us
    psum x1 -> x0, waiting for transfers between devices: 404 us -> none  [local(): filt_grad, gain_grad = lax.psum((filt_local, gain_local), 'ctx')]
    psum x3 -> x0, blocking collectives: 188 us -> none  [the longest x1 137 us: local(): filt_grad, gain_grad = lax.psum((filt_local, gain_local), 'ctx')]
    all_to_all x0 -> x2, blocking collectives: none -> 47.2 us  [the longest x1 27.4 us: local(): parts = lax.all_to_all(chunks, 'ctx', 0, 0, tiled=True)]
    conv_general_dilated x4 -> x0, matrix products: 43.9 us -> none  [depthwise(): lax.conv_general_dilated(source, kernel[:, None, :], (1,), 'VALID', dimen...]
    pallas_call x0 -> x3, Pallas kernels: none -> 10.7 us  [the longest x1 4.11 us: local(): pl.pallas_call(out_kernel, grid=(steps,), in_specs=[wide, wide, wide, squ...]
    ppermute x3 -> x2, waiting for transfers between devices: 2.45 us -> 12.8 us  [shifted(): lax.ppermute(value, axis, [(source, source + steps) for source in range(f...]
    ppermute x3 -> x2, starting transfers between devices: 15 us -> 7.75 us  [shifted(): lax.ppermute(value, axis, [(source, source + steps) for source in range(f...]
  transfers between devices with their start and end apart: 4 -> 3, of which waited for: 2 -> 2; matrix products, arithmetic and copies ran while one was open for 2% -> 0% of each run, Pallas kernels for 0% -> 4%
where the time goes in v1:
time: 98.4 us; the launch traced here: 97.9 us
  blocking collectives  47.2 us (48%)
  starting transfers between devices  13 us (13%)
  waiting for transfers between devices  12.8 us (13%)
  Pallas kernels  10.7 us (11%)
  local copies, waits for them, and re-layouts  8.48 us (9%)
  other arithmetic  2.84 us (3%)
  between operations  2.8 us (3%)
    all_to_all x1, blocking collectives, local(): parts = lax.all_to_all(chunks, 'ctx', 0, 0, tiled=True)  27.4 us
    all_to_all x1, blocking collectives, local(): stats = lax.all_to_all(stats, 'hid', 0, 0, tiled=True)  19.8 us
    ppermute x2, waiting for transfers between devices, shifted(): lax.ppermute(value, axis, [(source, source + steps) for source in range(f...  12.8 us
    ppermute x2, starting transfers between devices, shifted(): lax.ppermute(value, axis, [(source, source + steps) for source in range(f...  7.75 us
    unnamed x31, local copies, waits for them, and re-layouts  6.28 us
    all_to_all x1, starting transfers between devices, local(): lax.all_to_all(jnp.broadcast_to(mine[None], parts.shape), 'ctx', 0, 0, ti...  5.28 us
    pallas_call x1, Pallas kernels, local(): pl.pallas_call(out_kernel, grid=(steps,), in_specs=[wide, wide, wide, squ...  4.11 us
    pallas_call x1, Pallas kernels, local(): pl.pallas_call(grad_kernel, grid=(steps,), in_specs=[wide, wide, wide, sq...  3.43 us
  transfers between devices with their start and end apart: 3, of which 2 were waited for; matrix products, arithmetic and copies ran while one was open for 0% of the time, Pallas kernels for 4%

profile of v1, /device:TPU:1, one launch (start us, length us, event | category | flops | bytes accessed | tf_op | source)
XLA Modules:
  0.0 97.9 jit_solution(6561819260024091457)
XLA Ops:
  0.6 1.2 %slice.23 = s32[1]{0:T(128)} slice(s32[128]{0:T(128)} %param.16), slice={[127:128]} | slice | bytes 8 | tf_op jit(solution)/shard_map/slice | solution.py:237
  3.8 0.0 copy-start.2
  3.8 0.6 copy-done.2
  4.5 0.6 compare_convert_fusion
  5.1 0.0 copy-start
  5.2 0.0 copy-start.1
  5.2 0.0 copy-start.5
  5.2 0.0 copy-start.8
  5.2 1.3 %fusion.1 = bf16[128,1024]{1,0:T(8,128)(2,1)S(1)} fusion(bf16[128,1024]{1,0:T(8,128)(2,1)} %v_ref.5, bf16[128,1024]{1,0:T(8,128)(2,1)} %k_ref.5, pred[128]{0:T(512)(128)(4,1)S(1)} %get-tuple-element.25, bf16[128]{0:T(256)(128)(2,1)S(1)} %get-tuple-element.24, bf16[]{:T(256)S(6)} %convert_element_type.72), kind=kLoop, calls=%fused_computation.6 | loop fusion | flops 786432 | bytes 786818 | tf_op jit(solution)/shard_map/jit(_where)/select_n | solution.py:237
  6.5 5.4 %collective-permute-start = (bf16[128,1024]{1,0:T(8,128)(2,1)S(1)}, bf16[128,1024]{1,0:T(8,128)(2,1)S(1)}, u32[]{:S(2)}, u32[]{:S(2)}) collective-permute-start(bf16[128,1024]{1,0:T(8,128)(2,1)S(1)} %fusion.1), channel_id=1, source_target_pairs={{0,8},{8,16},{16,24},{24,32},{32,40},{40,48},{48,56},{56,64},{64,7... | collective-permute-start | bytes 786440 | tf_op jit(solution)/shard_map/ppermute | solution.py:222
  11.9 3.8 %collective-permute-done.halo_ref = bf16[128,1024]{1,0:T(8,128)(2,1)S(1)} collective-permute-done((bf16[128,1024]{1,0:T(8,128)(2,1)S(1)}, bf16[128,1024]{1,0:T(8,128)(2,1)S(1)}, u32[]{:S(2)}, u32[]{:S(2)}) %collective-permute-start) | collective-permute-done | bytes 262176 | tf_op jit(solution)/shard_map/ppermute | solution.py:222
  15.6 0.0 copy-done
  15.6 0.0 copy-done.1
  15.6 0.0 copy-done.5
  15.7 0.0 copy-done.8
  15.7 0.0 copy-start.3
  15.7 1.0 %copy-done.3 = f32[128,1024]{1,0:T(8,128)S(1)} copy-done((f32[128,1024]{1,0:T(8,128)S(1)}, f32[128,1024]{1,0:T(8,128)}, u32[]{:S(2)}) %copy-start.3) | copy-done | bytes 524312
  16.7 0.0 copy-start.6
  16.7 0.9 copy-done.6
  17.7 0.0 copy-start.9
  17.7 0.9 copy-done.9
  18.6 0.0 copy-start.11
  18.6 0.9 copy-done.11
  19.5 0.0 copy-start.14
  19.5 0.9 copy-done.14
  20.4 3.1 %conv_stats.1 = (f32[128,1024]{1,0:T(8,128)S(1)}, f32[8,2,128]{2,1,0:T(2,128)S(1)}) custom-call(bf16[256,256]{1,0:T(8,128)(2,1)S(1)} %copy-done.11, bf16[256,256]{1,0:T(8,128)(2,1)S(1)} %copy-done.14, bf16[256,256]{1,0:T(8,128)(2,1)S(1)} %copy-done.9, s32[1,128]{1,0:T(1,128)S(1)} %bitcast.25, bf16[128,1024]{1,0:T(8,128)(2,1)S(1)} %copy-done, ...), custom_call_target="tpu_custom_call" | custom-call | flops 1073741824 | bytes 3145728 | tf_op jit(solution)/shard_map/conv_stats/pallas_call | solution.py:242
  23.5 19.8 %all_to_all.15.stats_ref = f32[8,2,128]{2,1,0:T(2,128)S(1)} all-to-all(f32[8,2,128]{2,1,0:T(2,128)S(1)} %get-tuple-element.16), channel_id=1, replica_groups=mesh['ctx'=64,'hid'=8] {'hid'}, dimensions={0} | all-to-all | bytes 16384 | tf_op jit(solution)/shard_map/all_to_all | solution.py:253
  43.3 3.4 %filter_grad.1 = (bf16[8,8,9,2,128]{4,3,2,1,0:T(2,128)(2,1)S(1)}, bf16[128,1024]{1,0:T(8,128)(2,1)S(1)}, bf16[128,1024]{1,0:T(8,128)(2,1)S(1)}) custom-call(bf16[256,256]{1,0:T(8,128)(2,1)S(1)} %copy-done.11, bf16[256,256]{1,0:T(8,128)(2,1)S(1)} %copy-done.14, bf16[256,256]{1,0:T(8,128)(2,1)S(1)} %copy-done.9, s32[1,128]{1,0:T(1,128)S(1)} %bitcast.26, ...), custom_call_target="tpu_custom_call" | custom-call | flops 1073741824 | bytes 3145728 | tf_op jit(solution)/shard_map/filter_grad/pallas_call | solution.py:256
  46.8 27.4 %all_to_all.16 = bf16[64,9,2,128]{3,2,1,0:T(2,128)(2,1)S(1)} all-to-all(bf16[64,9,2,128]{3,2,1,0:T(2,128)(2,1)S(1)} %bitcast.24), channel_id=1, replica_groups=mesh['ctx'=64,'hid'=8] {'ctx'}, dimensions={0} | all-to-all | bytes 589824 | tf_op jit(solution)/shard_map/all_to_all | solution.py:268
  74.2 0.0 copy-start.10
  74.2 0.0 copy-start.12
  74.2 0.0 copy-start.13
  74.2 0.3 convert_reduce_fusion
  74.5 0.0 copy-start.4
  74.5 0.9 broadcast_in_dim.16
  75.4 0.0 copy-start.7
  75.4 5.3 %all-to-all-start.2 = ((bf16[64,9,2,128]{3,2,1,0:T(2,128)(2,1)}), bf16[64,9,2,128]{3,2,1,0:T(2,128)(2,1)S(1)}, u32[]{:S(2)}, u32[]{:S(2)}) async-start(bf16[64,9,2,128]{3,2,1,0:T(2,128)(2,1)} %broadcast_in_dim.16), calls=%async_computation.2 | async-start | bytes 589824 | tf_op jit(solution)/shard_map/all_to_all | solution.py:287
  80.7 2.4 %collective-permute-start.1 = (bf16[128,1024]{1,0:T(8,128)(2,1)S(1)}, bf16[128,1024]{1,0:T(8,128)(2,1)S(1)}, u32[]{:S(2)}, u32[]{:S(2)}) collective-permute-start(bf16[128,1024]{1,0:T(8,128)(2,1)S(1)} %get-tuple-element.18), channel_id=1, source_target_pairs={{8,0},{16,8},{24,16},{32,24},{40,32},{48,40},{56,48},{64,56},{72,6... | collective-permute-start | bytes 786440 | tf_op jit(solution)/shard_map/ppermute | solution.py:222
  83.1 9.0 %collective-permute-done.1.tail_ref = bf16[128,1024]{1,0:T(8,128)(2,1)S(1)} collective-permute-done((bf16[128,1024]{1,0:T(8,128)(2,1)S(1)}, bf16[128,1024]{1,0:T(8,128)(2,1)S(1)}, u32[]{:S(2)}, u32[]{:S(2)}) %collective-permute-start.1) | collective-permute-done | bytes 262176 | tf_op jit(solution)/shard_map/ppermute | solution.py:222
  92.1 0.0 copy-done.10
  92.1 0.0 copy-done.12
  92.1 0.0 copy-done.13
  92.1 0.0 copy-done.4
  92.1 0.0 copy-done.7
  92.1 4.1 %input_grads.1 = (bf16[128,1024]{1,0:T(8,128)(2,1)}, bf16[128,1024]{1,0:T(8,128)(2,1)}, bf16[128,1024]{1,0:T(8,128)(2,1)}, bf16[128,1024]{1,0:T(8,128)(2,1)}) custom-call(bf16[256,256]{1,0:T(8,128)(2,1)S(1)} %copy-done.12, bf16[256,256]{1,0:T(8,128)(2,1)S(1)} %copy-done.13, bf16[256,256]{1,0:T(8,128)(2,1)S(1)} %copy-done.10, s32[1,128]{1,0:T(1,128)S(1)} %bitcast.27, ...), custom_call_target="tpu_custom_call" | custom-call | flops 1073741824 | bytes 4194304 | tf_op jit(solution)/shard_map/input_grads/pallas_call | solution.py:271
  96.2 0.0 all-to-all-done.2
  96.2 0.1 copy.24
  96.3 0.6 add_bitcast_fusion
  97.0 0.9 copy.23
  (7 shorter events, 0.1 us)
Async XLA Ops:
  3.8 0.7 copy-start.2
  5.1 10.5 %copy-start = (bf16[128,1024]{1,0:T(8,128)(2,1)S(1)}, bf16[128,1024]{1,0:T(8,128)(2,1)}, u32[]{:S(2)}) copy-start(bf16[128,1024]{1,0:T(8,128)(2,1)} %k_ref.5) | copy-start | bytes 786436
  5.2 10.5 %copy-start.1 = (bf16[128,1024]{1,0:T(8,128)(2,1)S(1)}, bf16[128,1024]{1,0:T(8,128)(2,1)}, u32[]{:S(2)}) copy-start(bf16[128,1024]{1,0:T(8,128)(2,1)} %v_ref.5) | copy-start | bytes 786436
  5.2 10.5 %copy-start.5 = (bf16[128,1024]{1,0:T(8,128)(2,1)S(1)}, bf16[128,1024]{1,0:T(8,128)(2,1)}, u32[]{:S(2)}) copy-start(bf16[128,1024]{1,0:T(8,128)(2,1)} %q_ref.5) | copy-start | bytes 786436
  5.2 10.5 %copy-start.8 = (f32[1024]{0:T(1024)S(1)}, f32[1024]{0:T(1024)}, u32[]{:S(2)}) copy-start(f32[1024]{0:T(1024)} %param.15) | copy-start | bytes 12292
  6.5 9.2 %collective-permute-start = (bf16[128,1024]{1,0:T(8,128)(2,1)S(1)}, bf16[128,1024]{1,0:T(8,128)(2,1)S(1)}, u32[]{:S(2)}, u32[]{:S(2)}) collective-permute-start(bf16[128,1024]{1,0:T(8,128)(2,1)S(1)} %fusion.1), channel_id=1, source_target_pairs={{0,8},{8,16},{16,24},{24,32},{32,40},{40,48},{48,56},{56,64},{64,7... | collective-permute-start | bytes 786440 | tf_op jit(solution)/shard_map/ppermute | solution.py:222
  15.7 1.0 %copy-start.3 = (f32[128,1024]{1,0:T(8,128)S(1)}, f32[128,1024]{1,0:T(8,128)}, u32[]{:S(2)}) copy-start(f32[128,1024]{1,0:T(8,128)} %filt_ref.3) | copy-start | bytes 1572868
  16.7 0.9 copy-start.6
  17.7 0.9 copy-start.9
  18.6 0.9 copy-start.11
  19.5 0.9 copy-start.14
  74.2 17.9 %copy-start.10 = (bf16[256,256]{1,0:T(8,128)(2,1)S(1)}, bf16[256,256]{1,0:T(8,128)(2,1)}, u32[]{:S(2)}) copy-start(bf16[256,256]{1,0:T(8,128)(2,1)} %constant.27.clone.back_ref) | copy-start | bytes 393220
  74.2 17.9 %copy-start.12 = (bf16[256,256]{1,0:T(8,128)(2,1)S(1)}, bf16[256,256]{1,0:T(8,128)(2,1)}, u32[]{:S(2)}) copy-start(bf16[256,256]{1,0:T(8,128)(2,1)} %constant.24.clone.own_ref) | copy-start | bytes 393220
  74.2 17.9 %copy-start.13 = (bf16[256,256]{1,0:T(8,128)(2,1)S(1)}, bf16[256,256]{1,0:T(8,128)(2,1)}, u32[]{:S(2)}) copy-start(bf16[256,256]{1,0:T(8,128)(2,1)} %constant.26.clone.right_ref) | copy-start | bytes 393220
  74.5 17.6 %copy-start.4 = (f32[128,1024]{1,0:T(8,128)S(1)}, f32[128,1024]{1,0:T(8,128)}, u32[]{:S(2)}) copy-start(f32[128,1024]{1,0:T(8,128)} %filt_ref.3) | copy-start | bytes 1572868
  75.4 16.7 %copy-start.7 = (bf16[128,1024]{1,0:T(8,128)(2,1)S(1)}, bf16[128,1024]{1,0:T(8,128)(2,1)}, u32[]{:S(2)}) copy-start(bf16[128,1024]{1,0:T(8,128)(2,1)} %g_ref.5) | copy-start | bytes 786436
  75.4 20.8 %all-to-all-start.2 = ((bf16[64,9,2,128]{3,2,1,0:T(2,128)(2,1)}), bf16[64,9,2,128]{3,2,1,0:T(2,128)(2,1)S(1)}, u32[]{:S(2)}, u32[]{:S(2)}) async-start(bf16[64,9,2,128]{3,2,1,0:T(2,128)(2,1)} %broadcast_in_dim.16), calls=%async_computation.2 | async-start | bytes 589824 | tf_op jit(solution)/shard_map/all_to_all | solution.py:287
  80.7 11.4 %collective-permute-start.1 = (bf16[128,1024]{1,0:T(8,128)(2,1)S(1)}, bf16[128,1024]{1,0:T(8,128)(2,1)S(1)}, u32[]{:S(2)}, u32[]{:S(2)}) collective-permute-start(bf16[128,1024]{1,0:T(8,128)(2,1)S(1)} %get-tuple-element.18), channel_id=1, source_target_pairs={{8,0},{16,8},{24,16},{32,24},{40,32},{48,40},{56,48},{64,56},{72,6... | collective-permute-start | bytes 786440 | tf_op jit(solution)/shard_map/ppermute | solution.py:222

commit v2 on v0

v2 whole, which is shorter than its diff:
```python
import jax
import jax.numpy as jnp
import ml_dtypes
import numpy as np
from jax import lax
from jax.experimental import pallas as pl
from jax.experimental.pallas import tpu as pltpu
from jax.sharding import PartitionSpec as P

C = 8192
ROWS = 128
FREQ = 128
BLOCK = 256


def split_const(matrix):
    high = matrix.astype(ml_dtypes.bfloat16)
    low = (matrix - high.astype(np.float64)).astype(ml_dtypes.bfloat16)
    return high, low


def transforms():
    omega = 2.0 * np.pi * (np.arange(FREQ) + 0.5) / (2 * FREQ)

    def at(positions):
        angle = omega[:, None] * positions[None, :]
        return np.concatenate([np.cos(angle), -np.sin(angle)], axis=0)

    here = np.arange(ROWS)
    own = at(here)
    left = at(here - ROWS)
    left[:, 0] = 0.0
    right = at(here + ROWS)
    right[:, -1] = 0.0
    own_hl = np.concatenate(split_const(own), axis=1)
    left_hl = np.concatenate(split_const(left), axis=1)
    right_hl = np.concatenate(split_const(right), axis=1)
    back_hl = np.concatenate(split_const(own.T / FREQ), axis=0)
    return np.stack([own_hl, back_hl, left_hl, right_hl])


def mm(a, b):
    return jnp.dot(a, b, preferred_element_type=jnp.float32)


def forward(matrix_hl, x):
    return mm(matrix_hl, jnp.concatenate([x, x], axis=0))


def forward_wide(matrix_hl, x):
    high = x.astype(jnp.bfloat16)
    low = (x - high.astype(jnp.float32)).astype(jnp.bfloat16)
    return forward(matrix_hl, high) + mm(matrix_hl[:, :ROWS], low)


def backward(back_hl, spectrum):
    high = spectrum.astype(jnp.bfloat16)
    low = (spectrum - high.astype(jnp.float32)).astype(jnp.bfloat16)
    both = mm(back_hl, high)
    return both[:ROWS] + both[ROWS:] + mm(back_hl[:ROWS], low)


def times(a, b):
    ar, ai, br, bi = a[:FREQ], a[FREQ:], b[:FREQ], b[FREQ:]
    return jnp.concatenate([ar * br - ai * bi, ar * bi + ai * br], axis=0)


def times_conj(a, b):
    ar, ai, br, bi = a[:FREQ], a[FREQ:], b[:FREQ], b[FREQ:]
    return jnp.concatenate([ar * br + ai * bi, ai * br - ar * bi], axis=0)


def down(row, width):
    square = jnp.broadcast_to(row, (ROWS, ROWS)).T
    return jnp.concatenate([square] * (width // ROWS), axis=1)


def first_doc(seg):
    return (seg == seg[:, :1]).astype(jnp.float32)


def last_doc(seg):
    return (seg == seg[:, ROWS - 1 :]).astype(jnp.float32)


def parity(seg):
    return (seg % 2).astype(jnp.float32)


def blocks(width):
    return [slice(i, i + BLOCK) for i in range(0, width, BLOCK)]


def lane_sum(x):
    return sum(x[:, i : i + ROWS] for i in range(0, x.shape[1], ROWS))


def fetch(pairs, sems):
    copies = [pltpu.make_async_copy(source, target, sems.at[i]) for i, (source, target) in enumerate(pairs)]
    for copy in copies:
        copy.start()
    return copies


def message_kernel(seg_hbm, k_hbm, v_hbm, seg_ref, prod_ref, message_ref, k_ref, v_ref, sems):
    parts = blocks(k_ref.shape[1])
    pairs = [(seg_hbm, seg_ref)]
    for at in parts:
        pairs += [(k_hbm.at[:, at], k_ref.at[:, at]), (v_hbm.at[:, at], v_ref.at[:, at])]
    copies = fetch(pairs, sems)
    copies[0].wait()
    seg = seg_ref[...]
    in_last = down(last_doc(seg), BLOCK)
    is_top = lax.broadcasted_iota(jnp.int32, (ROWS, BLOCK), 0) == 0
    mark = parity(seg[:, ROWS - 1 :])
    for i, at in enumerate(parts):
        copies[2 * i + 1].wait()
        copies[2 * i + 2].wait()
        prod = (k_ref[:, at].astype(jnp.float32) * v_ref[:, at].astype(jnp.float32)).astype(jnp.bfloat16)
        prod_ref[:, at] = prod
        message_ref[:, at] = jnp.where(is_top, mark, prod.astype(jnp.float32) * in_last).astype(jnp.bfloat16)


def own_kernel(dft_hbm, filt_hbm, q_hbm, g_hbm, gain_hbm, seg_ref, prod_ref, dft_ref, q_ref, g_ref, gain_ref, taps_ref, all_ref, rest_ref, conv_ref, filt_ref, sems):
    copies = fetch([(dft_hbm, dft_ref), (filt_hbm, filt_ref), (q_hbm, q_ref), (g_hbm, g_ref), (gain_hbm, gain_ref)], sems)
    in_first = down(first_doc(seg_ref[...]), BLOCK)
    outside = (1.0 - in_first).astype(jnp.bfloat16)
    copies[0].wait()
    copies[1].wait()
    own, back = dft_ref[0], dft_ref[1]
    for at in blocks(prod_ref.shape[1]):
        prod = prod_ref[:, at]
        taps = forward_wide(own, filt_ref[:, at])
        all_spec = forward(own, prod)
        rest_spec = forward(own, prod * outside)
        taps_ref[:, at] = taps
        all_ref[:, at] = all_spec
        rest_ref[:, at] = rest_spec
        conv_first = backward(back, times(all_spec, taps))
        conv_rest = backward(back, times(rest_spec, taps))
        conv_ref[:, at] = jnp.where(in_first > 0.5, conv_first, conv_rest)
    for copy in copies[2:]:
        copy.wait()


def halo_kernel(dft_ref, seg_ref, halo_ref, taps_ref, all_ref, own_conv_ref, q_ref, g_ref, gain_ref, conv_ref, spec_ref, stats_ref):
    seg = seg_ref[...]
    in_first = down(first_doc(seg), BLOCK)
    mark = parity(seg[:, :1])
    back, left = dft_ref[1], dft_ref[2]
    square, inner = 0.0, 0.0
    for at in blocks(q_ref.shape[1]):
        halo = halo_ref[:, at]
        joined = (halo[0:1].astype(jnp.float32) == mark).astype(jnp.float32)
        halo_spec = forward(left, halo) * joined
        spec_ref[:, at] = all_ref[:, at] + halo_spec
        conv = own_conv_ref[:, at] + in_first * backward(back, times(halo_spec, taps_ref[:, at]))
        conv_ref[:, at] = conv
        y = q_ref[:, at].astype(jnp.float32) * conv
        square += lane_sum(y * y)
        inner += lane_sum(g_ref[:, at].astype(jnp.float32) * gain_ref[:, at] * y)
    rows = jnp.concatenate([jnp.sum(square.T, axis=0, keepdims=True), jnp.sum(inner.T, axis=0, keepdims=True)], axis=0)
    stats_ref[...] = jnp.broadcast_to(rows[None], stats_ref.shape)


def scales(stats_ref):
    total = jnp.sum(stats_ref[...], axis=0)
    rinv = lax.rsqrt(total[0:1] / C + 1e-06)
    return down(rinv, BLOCK), down(rinv * rinv * rinv * total[1:2] / C, BLOCK)


def filter_kernel(dft_ref, seg_ref, stats_ref, conv_ref, spec_ref, rest_ref, q_ref, g_ref, gain_ref, chunk_ref, head_ref):
    rinv, slope = scales(stats_ref)
    seg = seg_ref[...]
    first = down(first_doc(seg), BLOCK).astype(jnp.bfloat16)
    is_end = lax.broadcasted_iota(jnp.int32, (ROWS, BLOCK), 0) == ROWS - 1
    mark = parity(seg[:, :1])
    own, back = dft_ref[0], dft_ref[1]
    for step, at in enumerate(blocks(q_ref.shape[1])):
        query = q_ref[:, at].astype(jnp.float32)
        up = g_ref[:, at].astype(jnp.float32)
        y = query * conv_ref[:, at]
        dy = rinv * (up * gain_ref[:, at]) - y * slope
        dconv = (dy * query).astype(jnp.bfloat16)
        d_first = dconv * first
        head_ref[:, at] = jnp.where(is_end, mark, d_first.astype(jnp.float32)).astype(jnp.bfloat16)
        first_spec = forward(own, d_first)
        rest_spec = forward(own, dconv - d_first)
        spectrum = times_conj(first_spec, spec_ref[:, at]) + times_conj(rest_spec, rest_ref[:, at])
        taps = backward(back, spectrum).astype(jnp.bfloat16)
        gain_sum = jnp.sum(up * y * rinv, axis=0, keepdims=True)
        gain_high = gain_sum.astype(jnp.bfloat16)
        gain_low = (gain_sum - gain_high.astype(jnp.float32)).astype(jnp.bfloat16)
        gain_both = jnp.concatenate([gain_high, gain_low], axis=0)
        for sub in range(BLOCK // ROWS):
            lanes = slice(sub * ROWS, (sub + 1) * ROWS)
            block = step * (BLOCK // ROWS) + sub
            for group in range(8):
                for pair in range(8):
                    row = group * 16 + pair * 2
                    chunk_ref[group, block, pair] = taps[row : row + 2, lanes]
                chunk_ref[group, block, 8] = gain_both[:, lanes]


def out_kernel(q_hbm, g_hbm, stats_ref, conv_ref, gain_ref, layer_ref, qg_ref, dconv_ref, q_ref, g_ref, sems):
    copies = fetch([(q_hbm, q_ref), (g_hbm, g_ref)], sems)
    rinv, slope = scales(stats_ref)
    for copy in copies:
        copy.wait()
    for at in blocks(q_ref.shape[1]):
        query, conv, gain = q_ref[:, at].astype(jnp.float32), conv_ref[:, at], gain_ref[:, at]
        y = query * conv
        dy = rinv * (g_ref[:, at].astype(jnp.float32) * gain) - y * slope
        layer_ref[:, at] = (y * rinv * gain).astype(jnp.bfloat16)
        qg_ref[:, at] = (dy * conv).astype(jnp.bfloat16)
        dconv_ref[:, at] = (dy * query).astype(jnp.bfloat16)


def input_kernel(k_hbm, v_hbm, dft_ref, seg_ref, dconv_ref, tail_ref, taps_ref, kg_ref, vg_ref, k_ref, v_ref, sems):
    copies = fetch([(k_hbm, k_ref), (v_hbm, v_ref)], sems)
    seg = seg_ref[...]
    in_last = down(last_doc(seg), BLOCK)
    in_first = down(first_doc(seg), BLOCK).astype(jnp.bfloat16)
    mark = parity(seg[:, ROWS - 1 :])
    own, back, right = dft_ref[0], dft_ref[1], dft_ref[3]
    for copy in copies:
        copy.wait()
    for at in blocks(k_ref.shape[1]):
        dconv, tail, taps = dconv_ref[:, at], tail_ref[:, at], taps_ref[:, at]
        joined = (tail[ROWS - 1 :].astype(jnp.float32) == mark).astype(jnp.float32)
        last_spec = forward(own, dconv) + forward(right, tail) * joined
        first_spec = forward(own, dconv * in_first)
        dprod_last = backward(back, times_conj(last_spec, taps))
        dprod_first = backward(back, times_conj(first_spec, taps))
        dprod = jnp.where(in_last > 0.5, dprod_last, dprod_first)
        kg_ref[:, at] = (dprod * v_ref[:, at].astype(jnp.float32)).astype(jnp.bfloat16)
        vg_ref[:, at] = (dprod * k_ref[:, at].astype(jnp.float32)).astype(jnp.bfloat16)


def total_kernel(parts_ref, mine_ref):
    total = jnp.sum(parts_ref[...].astype(jnp.float32), axis=0)
    gain = total[8, 0:1] + total[8, 1:2]
    gain_high = gain.astype(jnp.bfloat16)
    gain_low = (gain - gain_high.astype(jnp.float32)).astype(jnp.bfloat16)
    mine = jnp.concatenate([total[:8].astype(jnp.bfloat16), jnp.concatenate([gain_high, gain_low], axis=0)[None]], axis=0)
    mine_ref[...] = jnp.broadcast_to(mine[None], mine_ref.shape)


def gather_kernel(full_ref, filt_ref, gain_ref):
    for block in range(full_ref.shape[1]):
        lanes = slice(block * ROWS, (block + 1) * ROWS)
        for group in range(8):
            for pair in range(8):
                row = group * 16 + pair * 2
                filt_ref[row : row + 2, lanes] = full_ref[group, block, pair].astype(jnp.float32)
        gain = full_ref[0, block, 8].astype(jnp.float32)
        gain_ref[:, lanes] = gain[0:1] + gain[1:2]


def call(kernel, name, outs, flops, hbm, vmem, scratch=(), pinned=True):
    hbm = [pltpu.with_memory_space_constraint(a, pltpu.HBM) for a in hbm]
    args = (*hbm, *vmem)
    moved = sum(a.size * a.dtype.itemsize for a in args)
    here = pl.BlockSpec(memory_space=pltpu.VMEM)
    space = pltpu.VMEM if pinned else jax.ShapeDtypeStruct
    return pl.pallas_call(
        kernel,
        in_specs=[pl.BlockSpec(memory_space=pltpu.HBM)] * len(hbm) + [here] * len(vmem),
        out_specs=[here] * len(outs),
        out_shape=[space(shape, dtype) for shape, dtype in outs],
        scratch_shapes=scratch,
        compiler_params=pltpu.CompilerParams(vmem_limit_bytes=32 * 1024 * 1024),
        cost_estimate=pl.CostEstimate(flops=flops, bytes_accessed=moved, transcendentals=0),
        name=name,
    )(*args)


def shifted(value, axis, steps):
    count = lax.axis_size(axis)
    first, last = (max(0, -steps), min(count, count - steps))
    return lax.ppermute(value, axis, [(source, source + steps) for source in range(first, last)])


def local(q_act, k_act, v_act, filt, gain, segments, grad_out):
    width = q_act.shape[1]
    n_ctx, n_hid = lax.axis_size("ctx"), lax.axis_size("hid")
    dft = jnp.asarray(transforms())
    seg = segments.reshape(1, ROWS)
    gain_row = gain.reshape(1, width)
    act = ((ROWS, width), jnp.bfloat16)
    wide = ((ROWS, width), jnp.float32)
    spec = ((2 * FREQ, width), jnp.float32)
    unit = 2**27

    row = ((1, width), jnp.float32)
    sems = pltpu.SemaphoreType.DMA((1 + 2 * (width // BLOCK),))
    mine = pltpu.VMEM((ROWS, width), jnp.bfloat16)
    seg, prod, message = call(
        message_kernel, "message", [((1, ROWS), jnp.int32), act, act], 2**18, (seg, k_act, v_act), (), [mine, mine, sems]
    )
    halo = shifted(message, "ctx", 1)
    dft, q_here, g_here, gain_here, taps, all_spec, rest_spec, own_conv = call(
        own_kernel,
        "own_conv",
        [(dft.shape, dft.dtype), act, act, row, spec, spec, spec, wide],
        8 * unit,
        (dft, filt, q_act, grad_out, gain_row),
        (seg, prod),
        [pltpu.VMEM(filt.shape, filt.dtype), pltpu.SemaphoreType.DMA((5,))],
    )
    conv, all_spec, stats = call(
        halo_kernel,
        "halo_conv",
        [wide, spec, ((n_hid, 2, ROWS), jnp.float32)],
        3 * unit,
        (),
        (dft, seg, halo, taps, all_spec, own_conv, q_here, g_here, gain_here),
    )
    stats = lax.all_to_all(stats, "hid", 0, 0, tiled=True)

    groups = (8, width // ROWS, 9, 2, ROWS)
    chunks, head = call(
        filter_kernel,
        "filter_grad",
        [(groups, jnp.bfloat16), act],
        5 * unit,
        (),
        (dft, seg, stats, conv, all_spec, rest_spec, q_here, g_here, gain_here),
    )
    parts = lax.all_to_all(chunks.reshape(n_ctx, 9, 2, ROWS), "ctx", 0, 0, tiled=True)
    parts, head = lax.optimization_barrier((parts, head))
    (total,) = call(total_kernel, "total", [(parts.shape, parts.dtype)], 2**18, (), (parts,))
    full = lax.all_to_all(total, "ctx", 0, 0, tiled=True)
    tail = shifted(head, "ctx", -1)
    pair = [mine, mine, pltpu.SemaphoreType.DMA((2,))]
    layer_out, q_grad, dconv = call(
        out_kernel, "out_grads", [act] * 3, 2**20, (q_act, grad_out), (stats, conv, gain_here), pair, False
    )
    k_grad, v_grad = call(
        input_kernel, "input_grads", [act, act], 6 * unit, (k_act, v_act), (dft, seg, dconv, tail, taps), pair, False
    )
    filt_grad, gain_grad = call(
        gather_kernel, "gather", [wide, row], 2**18, (), (full.reshape(groups),), (), False
    )
    return (layer_out, q_grad, k_grad, v_grad, filt_grad, gain_grad.reshape(width))


def solution(mesh):
    in_specs = (
        P("ctx", "hid"),
        P("ctx", "hid"),
        P("ctx", "hid"),
        P(None, "hid"),
        P("hid"),
        P("ctx"),
        P("ctx", "hid"),
    )
    out_specs = (
        P("ctx", "hid"),
        P("ctx", "hid"),
        P("ctx", "hid"),
        P("ctx", "hid"),
        P(None, "hid"),
        P("hid"),
    )
    return jax.shard_map(local, mesh=mesh, in_specs=in_specs, out_specs=out_specs, check_vma=False)
```

time: 688 us -> 83.6 us (0.12)
  waiting for transfers between devices: 407 us -> 7.63 us
  blocking collectives: 188 us -> 47.2 us
  matrix products: 43.9 us -> 0 us
  Pallas kernels: 0 us -> 14.7 us
  between operations: 14.3 us -> 0.71 us
  other arithmetic: 10.3 us -> 0 us
  local copies, waits for them, and re-layouts: 9.31 us -> 0 us
    psum x1 -> x0, waiting for transfers between devices: 404 us -> none  [local(): filt_grad, gain_grad = lax.psum((filt_local, gain_local), 'ctx')]
    psum x3 -> x0, blocking collectives: 188 us -> none  [the longest x1 137 us: local(): filt_grad, gain_grad = lax.psum((filt_local, gain_local), 'ctx')]
    all_to_all x0 -> x2, blocking collectives: none -> 47.2 us  [the longest x1 27.4 us: local(): lax.all_to_all(chunks.reshape(n_ctx, 9, 2, ROWS), 'ctx', 0, 0, tiled=True)]
    conv_general_dilated x4 -> x0, matrix products: 43.9 us -> none  [depthwise(): lax.conv_general_dilated(source, kernel[:, None, :], (1,), 'VALID', dimen...]
    pallas_call x0 -> x8, Pallas kernels: none -> 14.7 us  [call(): pl.pallas_call(kernel, in_specs=[pl.BlockSpec(memory_space=pltpu.HBM)] *...]
    ppermute x3 -> x2, starting transfers between devices: 15 us -> 7.75 us  [shifted(): lax.ppermute(value, axis, [(source, source + steps) for source in range(f...]
  transfers between devices with their start and end apart: 4 -> 3, of which waited for: 2 -> 2; matrix products, arithmetic and copies ran while one was open for 2% -> 0% of each run, Pallas kernels for 0% -> 10%
where the time goes in v2:
time: 83.6 us; the launch traced here: 83.2 us
  blocking collectives  47.2 us (56%)
  Pallas kernels  14.7 us (18%)
  starting transfers between devices  12.9 us (15%)
  waiting for transfers between devices  7.63 us (9%)
    all_to_all x1, blocking collectives, local(): lax.all_to_all(chunks.reshape(n_ctx, 9, 2, ROWS), 'ctx', 0, 0, tiled=True)  27.4 us
    all_to_all x1, blocking collectives, local(): stats = lax.all_to_all(stats, 'hid', 0, 0, tiled=True)  19.8 us
    pallas_call x8, Pallas kernels, call(): pl.pallas_call(kernel, in_specs=[pl.BlockSpec(memory_space=pltpu.HBM)] *...  14.7 us
    ppermute x2, starting transfers between devices, shifted(): lax.ppermute(value, axis, [(source, source + steps) for source in range(f...  7.75 us
    ppermute x2, waiting for transfers between devices, shifted(): lax.ppermute(value, axis, [(source, source + steps) for source in range(f...  7.63 us
    all_to_all x1, starting transfers between devices, local(): full = lax.all_to_all(total, 'ctx', 0, 0, tiled=True)  5.15 us
  transfers between devices with their start and end apart: 3, of which 2 were waited for; matrix products, arithmetic and copies ran while one was open for 0% of the time, Pallas kernels for 10%

profile of v2, /device:TPU:1, one launch (start us, length us, event | category | flops | bytes accessed | tf_op | source)
XLA Modules:
  0.0 83.2 jit_solution(8713560140827431047)
XLA Ops:
  0.6 1.2 %message.1 = (s32[1,128]{1,0:T(1,128)S(1)}, bf16[128,1024]{1,0:T(8,128)(2,1)S(1)}, bf16[128,1024]{1,0:T(8,128)(2,1)S(1)}) custom-call(s32[1,128]{1,0:T(1,128)} %bitcast.7, bf16[128,1024]{1,0:T(8,128)(2,1)} %k_hbm.3, bf16[128,1024]{1,0:T(8,128)(2,1)} %v_hbm.3), custom_call_target="tpu_custom_call" | custom-call | flops 262144 | bytes 524800 | tf_op jit(solution)/shard_map/message/pallas_call | solution.py:266
  1.8 5.4 %collective-permute-start = (bf16[128,1024]{1,0:T(8,128)(2,1)S(1)}, bf16[128,1024]{1,0:T(8,128)(2,1)S(1)}, u32[]{:S(2)}, u32[]{:S(2)}) collective-permute-start(bf16[128,1024]{1,0:T(8,128)(2,1)S(1)} %get-tuple-element.34), channel_id=1, source_target_pairs={{0,8},{8,16},{16,24},{24,32},{32,40},{40,48},{48,56},{56,64},{64,7... | collective-permute-start | bytes 786440 | tf_op jit(solution)/shard_map/ppermute | solution.py:281
  7.2 3.1 %own_conv.1 = (bf16[4,256,256]{2,1,0:T(8,128)(2,1)S(1)}, bf16[128,1024]{1,0:T(8,128)(2,1)S(1)}, bf16[128,1024]{1,0:T(8,128)(2,1)S(1)}, f32[1,1024]{1,0:T(1,128)S...) custom-call(bf16[4,256,256]{2,1,0:T(8,128)(2,1)} %constant.2.clone.d, ...), custom_call_target="tpu_custom_call" | custom-call | flops 1073741824 | bytes 1839616 | tf_op jit(solution)/shard_map/own_conv/pallas_call | solution.py:266
  10.4 0.7 collective-permute-done.halo_ref
  11.0 1.2 %halo_conv.1 = (f32[128,1024]{1,0:T(8,128)S(1)}, f32[256,1024]{1,0:T(8,128)S(1)}, f32[8,2,128]{2,1,0:T(2,128)S(1)}) custom-call(bf16[4,256,256]{2,1,0:T(8,128)(2,1)S(1)} %get-tuple-element.33.dft_ref, s32[1,128]{1,0:T(1,128)S(1)} %get-tuple-element.31.seg_ref, bf16[128,1024]{1,0:T(8,128)(2,1)S(1)} %collective-permute-done.halo_ref, ...), custom_call_target="tpu_custom_call" | custom-call | flops 402653184 | bytes 3936768 | tf_op jit(solution)/shard_map/halo_conv/pallas_call | solution.py:266
  12.3 19.8 %all_to_all.15.stats_ref = f32[8,2,128]{2,1,0:T(2,128)S(1)} all-to-all(f32[8,2,128]{2,1,0:T(2,128)S(1)} %get-tuple-element.41), channel_id=1, replica_groups=mesh['ctx'=64,'hid'=8] {'hid'}, dimensions={0} | all-to-all | bytes 16384 | tf_op jit(solution)/shard_map/all_to_all | solution.py:319
  32.1 1.5 %filter_grad.1 = (bf16[8,8,9,2,128]{4,3,2,1,0:T(2,128)(2,1)S(1)}, bf16[128,1024]{1,0:T(8,128)(2,1)S(1)}) custom-call(bf16[4,256,256]{2,1,0:T(8,128)(2,1)S(1)} %get-tuple-element.33.dft_ref, s32[1,128]{1,0:T(1,128)S(1)} %get-tuple-element.31.seg_ref, f32[8,2,128]{2,1,0:T(2,128)S(1)} %all_to_all.15.stats_ref, f32[128,1024]{1,0:T(8,128)S(1)} %get-tuple-element.42.conv_ref, ...), custom_call_target="tpu_custom_call" | custom-call | flops 671088640 | bytes 3682816 | tf_op jit(solution)/shard_map/filter_grad/pallas_call | solution.py:266
  33.6 27.4 %all_to_all.16.parts_ref = bf16[64,9,2,128]{3,2,1,0:T(2,128)(2,1)S(1)} all-to-all(bf16[64,9,2,128]{3,2,1,0:T(2,128)(2,1)S(1)} %bitcast.6), channel_id=1, replica_groups=mesh['ctx'=64,'hid'=8] {'ctx'}, dimensions={0} | all-to-all | bytes 589824 | tf_op jit(solution)/shard_map/all_to_all | solution.py:330
  61.0 1.1 %total.1 = bf16[64,9,2,128]{3,2,1,0:T(2,128)(2,1)} custom-call(bf16[64,9,2,128]{3,2,1,0:T(2,128)(2,1)S(1)} %all_to_all.16.parts_ref), custom_call_target="tpu_custom_call" | custom-call | flops 262144 | bytes 294912 | tf_op jit(solution)/shard_map/total/pallas_call | solution.py:266
  62.1 5.2 %all-to-all-start.2 = ((bf16[64,9,2,128]{3,2,1,0:T(2,128)(2,1)}), bf16[64,9,2,128]{3,2,1,0:T(2,128)(2,1)S(1)}, u32[]{:S(2)}, u32[]{:S(2)}) async-start(bf16[64,9,2,128]{3,2,1,0:T(2,128)(2,1)} %total.1), calls=%async_computation.2 | async-start | bytes 589824 | tf_op jit(solution)/shard_map/all_to_all | solution.py:333
  67.3 2.4 %collective-permute-start.1 = (bf16[128,1024]{1,0:T(8,128)(2,1)S(1)}, bf16[128,1024]{1,0:T(8,128)(2,1)S(1)}, u32[]{:S(2)}, u32[]{:S(2)}) collective-permute-start(bf16[128,1024]{1,0:T(8,128)(2,1)S(1)} %get-tuple-element.50), channel_id=1, source_target_pairs={{8,0},{16,8},{24,16},{32,24},{40,32},{48,40},{56,48},{64,56},{72,6... | collective-permute-start | bytes 786440 | tf_op jit(solution)/shard_map/ppermute | solution.py:281
  69.6 2.0 %out_grads.1 = (bf16[128,1024]{1,0:T(8,128)(2,1)}, bf16[128,1024]{1,0:T(8,128)(2,1)}, bf16[128,1024]{1,0:T(8,128)(2,1)S(1)}) custom-call(bf16[128,1024]{1,0:T(8,128)(2,1)} %q_hbm.3, bf16[128,1024]{1,0:T(8,128)(2,1)} %g_hbm.3, f32[8,2,128]{2,1,0:T(2,128)S(1)} %all_to_all.15.stats_ref, f32[128,1024]{1,0:T(8,128)S(1)} %get-tuple-element.42.conv_ref, ...), custom_call_target="tpu_custom_call" | custom-call | flops 1048576 | bytes 1060864 | tf_op jit(solution)/shard_map/out_grads/pallas_call | solution.py:266
  71.7 7.0 %collective-permute-done.1.tail_ref = bf16[128,1024]{1,0:T(8,128)(2,1)S(1)} collective-permute-done((bf16[128,1024]{1,0:T(8,128)(2,1)S(1)}, bf16[128,1024]{1,0:T(8,128)(2,1)S(1)}, u32[]{:S(2)}, u32[]{:S(2)}) %collective-permute-start.1) | collective-permute-done | bytes 262176 | tf_op jit(solution)/shard_map/ppermute | solution.py:281
  78.6 3.6 %input_grads.1 = (bf16[128,1024]{1,0:T(8,128)(2,1)}, bf16[128,1024]{1,0:T(8,128)(2,1)}) custom-call(bf16[128,1024]{1,0:T(8,128)(2,1)} %k_hbm.3, bf16[128,1024]{1,0:T(8,128)(2,1)} %v_hbm.3, bf16[4,256,256]{2,1,0:T(8,128)(2,1)S(1)} %get-tuple-element.33.dft_ref, s32[1,128]{1,0:T(1,128)S(1)} %get-tuple-element.31.seg_ref, ...), custom_call_target="tpu_custom_call" | custom-call | flops 805306368 | bytes 2621952 | tf_op jit(solution)/shard_map/input_grads/pallas_call | solution.py:266
  82.2 0.0 all-to-all-done.2
  82.2 1.0 %gather.1 = (f32[128,1024]{1,0:T(8,128)}, f32[1,1024]{1,0:T(1,128)}) custom-call(bf16[8,8,9,2,128]{4,3,2,1,0:T(2,128)(2,1)S(1)} %bitcast.5), custom_call_target="tpu_custom_call" | custom-call | flops 262144 | bytes 294912 | tf_op jit(solution)/shard_map/gather/pallas_call | solution.py:266
Async XLA Ops:
  1.8 9.2 %collective-permute-start = (bf16[128,1024]{1,0:T(8,128)(2,1)S(1)}, bf16[128,1024]{1,0:T(8,128)(2,1)S(1)}, u32[]{:S(2)}, u32[]{:S(2)}) collective-permute-start(bf16[128,1024]{1,0:T(8,128)(2,1)S(1)} %get-tuple-element.34), channel_id=1, source_target_pairs={{0,8},{8,16},{16,24},{24,32},{32,40},{40,48},{48,56},{56,64},{64,7... | collective-permute-start | bytes 786440 | tf_op jit(solution)/shard_map/ppermute | solution.py:281
  62.1 20.1 %all-to-all-start.2 = ((bf16[64,9,2,128]{3,2,1,0:T(2,128)(2,1)}), bf16[64,9,2,128]{3,2,1,0:T(2,128)(2,1)S(1)}, u32[]{:S(2)}, u32[]{:S(2)}) async-start(bf16[64,9,2,128]{3,2,1,0:T(2,128)(2,1)} %total.1), calls=%async_computation.2 | async-start | bytes 589824 | tf_op jit(solution)/shard_map/all_to_all | solution.py:333
  67.3 11.4 %collective-permute-start.1 = (bf16[128,1024]{1,0:T(8,128)(2,1)S(1)}, bf16[128,1024]{1,0:T(8,128)(2,1)S(1)}, u32[]{:S(2)}, u32[]{:S(2)}) collective-permute-start(bf16[128,1024]{1,0:T(8,128)(2,1)S(1)} %get-tuple-element.50), channel_id=1, source_target_pairs={{8,0},{16,8},{24,16},{32,24},{40,32},{48,40},{56,48},{64,56},{72,6... | collective-permute-start | bytes 786440 | tf_op jit(solution)/shard_map/ppermute | solution.py:281

commit v3 on v2

--- a/solution.py
+++ b/solution.py
@@ -202,37 +202,40 @@
                 chunk_ref[group, block, 8] = gain_both[:, lanes]
 
 
-def out_kernel(q_hbm, g_hbm, stats_ref, conv_ref, gain_ref, layer_ref, qg_ref, dconv_ref, q_ref, g_ref, sems):
-    copies = fetch([(q_hbm, q_ref), (g_hbm, g_ref)], sems)
+def out_kernel(q_hbm, g_hbm, k_hbm, v_hbm, dft_ref, seg_ref, stats_ref, conv_ref, taps_ref, gain_ref, layer_ref, qg_ref, dprod_ref, k_ref, v_ref, q_ref, g_ref, sems):
+    copies = fetch([(q_hbm, q_ref), (g_hbm, g_ref), (k_hbm, k_ref), (v_hbm, v_ref)], sems)
     rinv, slope = scales(stats_ref)
-    for copy in copies:
-        copy.wait()
+    seg = seg_ref[...]
+    in_last = down(last_doc(seg), BLOCK)
+    in_first = down(first_doc(seg), BLOCK).astype(jnp.bfloat16)
+    own, back = dft_ref[0], dft_ref[1]
+    copies[0].wait()
+    copies[1].wait()
     for at in blocks(q_ref.shape[1]):
         query, conv, gain = q_ref[:, at].astype(jnp.float32), conv_ref[:, at], gain_ref[:, at]
         y = query * conv
         dy = rinv * (g_ref[:, at].astype(jnp.float32) * gain) - y * slope
         layer_ref[:, at] = (y * rinv * gain).astype(jnp.bfloat16)
         qg_ref[:, at] = (dy * conv).astype(jnp.bfloat16)
-        dconv_ref[:, at] = (dy * query).astype(jnp.bfloat16)
-
-
-def input_kernel(k_hbm, v_hbm, dft_ref, seg_ref, dconv_ref, tail_ref, taps_ref, kg_ref, vg_ref, k_ref, v_ref, sems):
-    copies = fetch([(k_hbm, k_ref), (v_hbm, v_ref)], sems)
+        dconv = (dy * query).astype(jnp.bfloat16)
+        taps = taps_ref[:, at]
+        dprod_last = backward(back, times_conj(forward(own, dconv), taps))
+        dprod_first = backward(back, times_conj(forward(own, dconv * in_first), taps))
+        dprod_ref[:, at] = jnp.where(in_last > 0.5, dprod_last, dprod_first)
+    copies[2].wait()
+    copies[3].wait()
+
+
+def input_kernel(dft_ref, seg_ref, dprod_ref, tail_ref, taps_ref, k_ref, v_ref, kg_ref, vg_ref):
     seg = seg_ref[...]
     in_last = down(last_doc(seg), BLOCK)
-    in_first = down(first_doc(seg), BLOCK).astype(jnp.bfloat16)
     mark = parity(seg[:, ROWS - 1 :])
-    own, back, right = dft_ref[0], dft_ref[1], dft_ref[3]
-    for copy in copies:
-        copy.wait()
+    back, right = dft_ref[1], dft_ref[3]
     for at in blocks(k_ref.shape[1]):
-        dconv, tail, taps = dconv_ref[:, at], tail_ref[:, at], taps_ref[:, at]
+        tail = tail_ref[:, at]
         joined = (tail[ROWS - 1 :].astype(jnp.float32) == mark).astype(jnp.float32)
-        last_spec = forward(own, dconv) + forward(right, tail) * joined
-        first_spec = forward(own, dconv * in_first)
-        dprod_last = backward(back, times_conj(last_spec, taps))
-        dprod_first = backward(back, times_conj(first_spec, taps))
-        dprod = jnp.where(in_last > 0.5, dprod_last, dprod_first)
+        tail_spec = forward(right, tail) * joined
+        dprod = dprod_ref[:, at] + in_last * backward(back, times_conj(tail_spec, taps_ref[:, at]))
         kg_ref[:, at] = (dprod * v_ref[:, at].astype(jnp.float32)).astype(jnp.bfloat16)
         vg_ref[:, at] = (dprod * k_ref[:, at].astype(jnp.float32)).astype(jnp.bfloat16)
 
@@ -332,12 +335,18 @@
     (total,) = call(total_kernel, "total", [(parts.shape, parts.dtype)], 2**18, (), (parts,))
     full = lax.all_to_all(total, "ctx", 0, 0, tiled=True)
     tail = shifted(head, "ctx", -1)
-    pair = [mine, mine, pltpu.SemaphoreType.DMA((2,))]
-    layer_out, q_grad, dconv = call(
-        out_kernel, "out_grads", [act] * 3, 2**20, (q_act, grad_out), (stats, conv, gain_here), pair, False
+    layer_out, q_grad, own_dprod, k_here, v_here = call(
+        out_kernel,
+        "out_grads",
+        [act, act, wide, act, act],
+        6 * unit,
+        (q_act, grad_out, k_act, v_act),
+        (dft, seg, stats, conv, taps, gain_here),
+        [mine, mine, pltpu.SemaphoreType.DMA((4,))],
+        False,
     )
     k_grad, v_grad = call(
-        input_kernel, "input_grads", [act, act], 6 * unit, (k_act, v_act), (dft, seg, dconv, tail, taps), pair, False
+        input_kernel, "input_grads", [act, act], 3 * unit, (), (dft, seg, own_dprod, tail, taps, k_here, v_here), (), False
     )
     filt_grad, gain_grad = call(
         gather_kernel, "gather", [wide, row], 2**18, (), (full.reshape(groups),), (), False

time: 83.6 us -> 81.9 us (0.980)
  waiting for transfers between devices: 7.63 us -> 6.02 us
    ppermute x2, waiting for transfers between devices: 7.63 us -> 6.01 us  [shifted(): lax.ppermute(value, axis, [(source, source + steps) for source in range(f...]
  transfers between devices with their start and end apart: 3 -> 3, of which waited for: 2 -> 2; matrix products, arithmetic and copies ran while one was open for 0% -> 0% of each run, Pallas kernels for 10% -> 11%
where the time goes in v3:
time: 81.9 us; the launch traced here: 81.5 us
  blocking collectives  47.2 us (58%)
  Pallas kernels  14.7 us (18%)
  starting transfers between devices  12.9 us (16%)
  waiting for transfers between devices  6.02 us (7%)
    all_to_all x1, blocking collectives, local(): lax.all_to_all(chunks.reshape(n_ctx, 9, 2, ROWS), 'ctx', 0, 0, tiled=True)  27.4 us
    all_to_all x1, blocking collectives, local(): stats = lax.all_to_all(stats, 'hid', 0, 0, tiled=True)  19.8 us
    pallas_call x8, Pallas kernels, call(): pl.pallas_call(kernel, in_specs=[pl.BlockSpec(memory_space=pltpu.HBM)] *...  14.7 us
    ppermute x2, starting transfers between devices, shifted(): lax.ppermute(value, axis, [(source, source + steps) for source in range(f...  7.75 us
    ppermute x2, waiting for transfers between devices, shifted(): lax.ppermute(value, axis, [(source, source + steps) for source in range(f...  6.01 us
    all_to_all x1, starting transfers between devices, local(): full = lax.all_to_all(total, 'ctx', 0, 0, tiled=True)  5.15 us
  transfers between devices with their start and end apart: 3, of which 2 were waited for; matrix products, arithmetic and copies ran while one was open for 0% of the time, Pallas kernels for 11%

profile of v3, /device:TPU:1, one launch (start us, length us, event | category | flops | bytes accessed | tf_op | source)
XLA Modules:
  0.0 81.5 jit_solution(18248128112786127604)
XLA Ops:
  0.6 1.2 %message.1 = (s32[1,128]{1,0:T(1,128)S(1)}, bf16[128,1024]{1,0:T(8,128)(2,1)S(1)}, bf16[128,1024]{1,0:T(8,128)(2,1)S(1)}) custom-call(s32[1,128]{1,0:T(1,128)} %bitcast.7, bf16[128,1024]{1,0:T(8,128)(2,1)} %k_hbm.3, bf16[128,1024]{1,0:T(8,128)(2,1)} %v_hbm.3), custom_call_target="tpu_custom_call" | custom-call | flops 262144 | bytes 524800 | tf_op jit(solution)/shard_map/message/pallas_call | solution.py:269
  1.8 5.4 %collective-permute-start = (bf16[128,1024]{1,0:T(8,128)(2,1)S(1)}, bf16[128,1024]{1,0:T(8,128)(2,1)S(1)}, u32[]{:S(2)}, u32[]{:S(2)}) collective-permute-start(bf16[128,1024]{1,0:T(8,128)(2,1)S(1)} %get-tuple-element.36), channel_id=1, source_target_pairs={{0,8},{8,16},{16,24},{24,32},{32,40},{40,48},{48,56},{56,64},{64,7... | collective-permute-start | bytes 786440 | tf_op jit(solution)/shard_map/ppermute | solution.py:284
  7.2 3.1 %own_conv.1 = (bf16[4,256,256]{2,1,0:T(8,128)(2,1)S(1)}, bf16[128,1024]{1,0:T(8,128)(2,1)S(1)}, bf16[128,1024]{1,0:T(8,128)(2,1)S(1)}, f32[1,1024]{1,0:T(1,128)S...) custom-call(bf16[4,256,256]{2,1,0:T(8,128)(2,1)} %constant.2.clone.d, ...), custom_call_target="tpu_custom_call" | custom-call | flops 1073741824 | bytes 1839616 | tf_op jit(solution)/shard_map/own_conv/pallas_call | solution.py:269
  10.4 0.7 collective-permute-done.halo_ref
  11.0 1.2 %halo_conv.1 = (f32[128,1024]{1,0:T(8,128)S(1)}, f32[256,1024]{1,0:T(8,128)S(1)}, f32[8,2,128]{2,1,0:T(2,128)S(1)}) custom-call(bf16[4,256,256]{2,1,0:T(8,128)(2,1)S(1)} %get-tuple-element.35.dft_ref, s32[1,128]{1,0:T(1,128)S(1)} %get-tuple-element.33.seg_ref, bf16[128,1024]{1,0:T(8,128)(2,1)S(1)} %collective-permute-done.halo_ref, ...), custom_call_target="tpu_custom_call" | custom-call | flops 402653184 | bytes 3936768 | tf_op jit(solution)/shard_map/halo_conv/pallas_call | solution.py:269
  12.3 19.8 %all_to_all.15.stats_ref = f32[8,2,128]{2,1,0:T(2,128)S(1)} all-to-all(f32[8,2,128]{2,1,0:T(2,128)S(1)} %get-tuple-element.43), channel_id=1, replica_groups=mesh['ctx'=64,'hid'=8] {'hid'}, dimensions={0} | all-to-all | bytes 16384 | tf_op jit(solution)/shard_map/all_to_all | solution.py:322
  32.1 1.5 %filter_grad.1 = (bf16[8,8,9,2,128]{4,3,2,1,0:T(2,128)(2,1)S(1)}, bf16[128,1024]{1,0:T(8,128)(2,1)S(1)}) custom-call(bf16[4,256,256]{2,1,0:T(8,128)(2,1)S(1)} %get-tuple-element.35.dft_ref, s32[1,128]{1,0:T(1,128)S(1)} %get-tuple-element.33.seg_ref, f32[8,2,128]{2,1,0:T(2,128)S(1)} %all_to_all.15.stats_ref, f32[128,1024]{1,0:T(8,128)S(1)} %get-tuple-element.44.conv_ref, ...), custom_call_target="tpu_custom_call" | custom-call | flops 671088640 | bytes 3682816 | tf_op jit(solution)/shard_map/filter_grad/pallas_call | solution.py:269
  33.6 27.4 %all_to_all.16.parts_ref = bf16[64,9,2,128]{3,2,1,0:T(2,128)(2,1)S(1)} all-to-all(bf16[64,9,2,128]{3,2,1,0:T(2,128)(2,1)S(1)} %bitcast.6), channel_id=1, replica_groups=mesh['ctx'=64,'hid'=8] {'ctx'}, dimensions={0} | all-to-all | bytes 589824 | tf_op jit(solution)/shard_map/all_to_all | solution.py:333
  61.0 1.1 %total.1 = bf16[64,9,2,128]{3,2,1,0:T(2,128)(2,1)} custom-call(bf16[64,9,2,128]{3,2,1,0:T(2,128)(2,1)S(1)} %all_to_all.16.parts_ref), custom_call_target="tpu_custom_call" | custom-call | flops 262144 | bytes 294912 | tf_op jit(solution)/shard_map/total/pallas_call | solution.py:269
  62.1 5.2 %all-to-all-start.2 = ((bf16[64,9,2,128]{3,2,1,0:T(2,128)(2,1)}), bf16[64,9,2,128]{3,2,1,0:T(2,128)(2,1)S(1)}, u32[]{:S(2)}, u32[]{:S(2)}) async-start(bf16[64,9,2,128]{3,2,1,0:T(2,128)(2,1)} %total.1), calls=%async_computation.2 | async-start | bytes 589824 | tf_op jit(solution)/shard_map/all_to_all | solution.py:336
  67.3 2.4 %collective-permute-start.1 = (bf16[128,1024]{1,0:T(8,128)(2,1)S(1)}, bf16[128,1024]{1,0:T(8,128)(2,1)S(1)}, u32[]{:S(2)}, u32[]{:S(2)}) collective-permute-start(bf16[128,1024]{1,0:T(8,128)(2,1)S(1)} %get-tuple-element.52), channel_id=1, source_target_pairs={{8,0},{16,8},{24,16},{32,24},{40,32},{48,40},{56,48},{64,56},{72,6... | collective-permute-start | bytes 786440 | tf_op jit(solution)/shard_map/ppermute | solution.py:284
  69.6 3.6 %out_grads.1 = (bf16[128,1024]{1,0:T(8,128)(2,1)}, bf16[128,1024]{1,0:T(8,128)(2,1)}, f32[128,1024]{1,0:T(8,128)S(1)}, bf16[128,1024]{1,0:T(8,128)(2,1)S(1)}, bf16[128,1024]{1,0:T(8,128)(2,1)S(1)}) custom-call(bf16[128,1024]{1,0:T(8,128)(2,1)} %q_hbm.3, bf16[128,1024]{1,0:T(8,128)(2,1)} %g_hbm.3, bf16[128,1024]{1,0:T(8,128)(2,1)} %k_hbm.3, ...), custom_call_target="tpu_custom_call" | custom-call | flops 805306368 | bytes 3158528 | tf_op jit(solution)/shard_map/out_grads/pallas_call | solution.py:269
  73.3 5.4 %collective-permute-done.1.tail_ref = bf16[128,1024]{1,0:T(8,128)(2,1)S(1)} collective-permute-done((bf16[128,1024]{1,0:T(8,128)(2,1)S(1)}, bf16[128,1024]{1,0:T(8,128)(2,1)S(1)}, u32[]{:S(2)}, u32[]{:S(2)}) %collective-permute-start.1) | collective-permute-done | bytes 262176 | tf_op jit(solution)/shard_map/ppermute | solution.py:284
  78.6 1.9 %input_grads.1 = (bf16[128,1024]{1,0:T(8,128)(2,1)}, bf16[128,1024]{1,0:T(8,128)(2,1)}) custom-call(bf16[4,256,256]{2,1,0:T(8,128)(2,1)S(1)} %get-tuple-element.35.dft_ref, s32[1,128]{1,0:T(1,128)S(1)} %get-tuple-element.33.seg_ref, f32[128,1024]{1,0:T(8,128)S(1)} %get-tuple-element.47.dprod_ref, bf16[128,1024]{1,0:T(8,128)(2,1)S(1)} %collective-permute-done.1.tail_ref, ...), custom_call_target="tpu_custom_call" | custom-call | flops 402653184 | bytes 2884096 | tf_op jit(solution)/shard_map/input_grads/pallas_call | solution.py:269
  80.5 0.0 all-to-all-done.2
  80.5 1.0 %gather.1 = (f32[128,1024]{1,0:T(8,128)}, f32[1,1024]{1,0:T(1,128)}) custom-call(bf16[8,8,9,2,128]{4,3,2,1,0:T(2,128)(2,1)S(1)} %bitcast.5), custom_call_target="tpu_custom_call" | custom-call | flops 262144 | bytes 294912 | tf_op jit(solution)/shard_map/gather/pallas_call | solution.py:269
Async XLA Ops:
  1.8 9.2 %collective-permute-start = (bf16[128,1024]{1,0:T(8,128)(2,1)S(1)}, bf16[128,1024]{1,0:T(8,128)(2,1)S(1)}, u32[]{:S(2)}, u32[]{:S(2)}) collective-permute-start(bf16[128,1024]{1,0:T(8,128)(2,1)S(1)} %get-tuple-element.36), channel_id=1, source_target_pairs={{0,8},{8,16},{16,24},{24,32},{32,40},{40,48},{48,56},{56,64},{64,7... | collective-permute-start | bytes 786440 | tf_op jit(solution)/shard_map/ppermute | solution.py:284
  62.1 18.4 %all-to-all-start.2 = ((bf16[64,9,2,128]{3,2,1,0:T(2,128)(2,1)}), bf16[64,9,2,128]{3,2,1,0:T(2,128)(2,1)S(1)}, u32[]{:S(2)}, u32[]{:S(2)}) async-start(bf16[64,9,2,128]{3,2,1,0:T(2,128)(2,1)} %total.1), calls=%async_computation.2 | async-start | bytes 589824 | tf_op jit(solution)/shard_map/all_to_all | solution.py:336
  67.3 11.4 %collective-permute-start.1 = (bf16[128,1024]{1,0:T(8,128)(2,1)S(1)}, bf16[128,1024]{1,0:T(8,128)(2,1)S(1)}, u32[]{:S(2)}, u32[]{:S(2)}) collective-permute-start(bf16[128,1024]{1,0:T(8,128)(2,1)S(1)} %get-tuple-element.52), channel_id=1, source_target_pairs={{8,0},{16,8},{24,16},{32,24},{40,32},{48,40},{56,48},{64,56},{72,6... | collective-permute-start | bytes 786440 | tf_op jit(solution)/shard_map/ppermute | solution.py:284

commit v4 on v3

--- a/solution.py
+++ b/solution.py
@@ -5,12 +5,17 @@
 from jax import lax
 from jax.experimental import pallas as pl
 from jax.experimental.pallas import tpu as pltpu
+from jax.sharding import Mesh
 from jax.sharding import PartitionSpec as P
 
 C = 8192
 ROWS = 128
 FREQ = 128
-BLOCK = 256
+BLOCK = 1024
+PART = 512
+COPIES = 4
+RUN = 8
+HID = ("x", "z_hi")
 
 
 def split_const(matrix):
@@ -87,8 +92,8 @@
     return (seg % 2).astype(jnp.float32)
 
 
-def blocks(width):
-    return [slice(i, i + BLOCK) for i in range(0, width, BLOCK)]
+def blocks(width, size=BLOCK):
+    return [slice(i, i + size) for i in range(0, width, size)]
 
 
 def lane_sum(x):
@@ -102,23 +107,34 @@
     return copies
 
 
-def message_kernel(seg_hbm, k_hbm, v_hbm, seg_ref, prod_ref, message_ref, k_ref, v_ref, sems):
-    parts = blocks(k_ref.shape[1])
+def compose(seg_hbm, k_hbm, v_hbm, seg_ref, prod_ref, message_ref, k_ref, v_ref, sems):
+    parts = blocks(k_ref.shape[1], PART)
     pairs = [(seg_hbm, seg_ref)]
     for at in parts:
         pairs += [(k_hbm.at[:, at], k_ref.at[:, at]), (v_hbm.at[:, at], v_ref.at[:, at])]
     copies = fetch(pairs, sems)
     copies[0].wait()
     seg = seg_ref[...]
-    in_last = down(last_doc(seg), BLOCK)
-    is_top = lax.broadcasted_iota(jnp.int32, (ROWS, BLOCK), 0) == 0
+    in_last = down(last_doc(seg), PART)
+    is_top = lax.broadcasted_iota(jnp.int32, (ROWS, PART), 0) == 0
     mark = parity(seg[:, ROWS - 1 :])
     for i, at in enumerate(parts):
         copies[2 * i + 1].wait()
         copies[2 * i + 2].wait()
         prod = (k_ref[:, at].astype(jnp.float32) * v_ref[:, at].astype(jnp.float32)).astype(jnp.bfloat16)
-        prod_ref[:, at] = prod
+        if prod_ref is not None:
+            prod_ref[:, at] = prod
         message_ref[:, at] = jnp.where(is_top, mark, prod.astype(jnp.float32) * in_last).astype(jnp.bfloat16)
+
+
+def far_kernel(seg_hbm, k_hbm, v_hbm, message_ref, seg_ref, k_ref, v_ref, sems):
+    @pl.when(lax.axis_index("ctx") % RUN == RUN - 1)
+    def _():
+        compose(seg_hbm, k_hbm, v_hbm, seg_ref, None, message_ref, k_ref, v_ref, sems)
+
+
+def message_kernel(seg_hbm, k_hbm, v_hbm, seg_ref, prod_ref, message_ref, k_ref, v_ref, sems):
+    compose(seg_hbm, k_hbm, v_hbm, seg_ref, prod_ref, message_ref, k_ref, v_ref, sems)
 
 
 def own_kernel(dft_hbm, filt_hbm, q_hbm, g_hbm, gain_hbm, seg_ref, prod_ref, dft_ref, q_ref, g_ref, gain_ref, taps_ref, all_ref, rest_ref, conv_ref, filt_ref, sems):
@@ -143,14 +159,14 @@
         copy.wait()
 
 
-def halo_kernel(dft_ref, seg_ref, halo_ref, taps_ref, all_ref, own_conv_ref, q_ref, g_ref, gain_ref, conv_ref, spec_ref, stats_ref):
+def halo_kernel(dft_ref, seg_ref, near_ref, far_ref, taps_ref, all_ref, own_conv_ref, q_ref, g_ref, gain_ref, conv_ref, spec_ref, stats_ref):
     seg = seg_ref[...]
     in_first = down(first_doc(seg), BLOCK)
     mark = parity(seg[:, :1])
     back, left = dft_ref[1], dft_ref[2]
     square, inner = 0.0, 0.0
     for at in blocks(q_ref.shape[1]):
-        halo = halo_ref[:, at]
+        halo = near_ref[:, at] + far_ref[:, at]
         joined = (halo[0:1].astype(jnp.float32) == mark).astype(jnp.float32)
         halo_spec = forward(left, halo) * joined
         spec_ref[:, at] = all_ref[:, at] + halo_spec
@@ -163,14 +179,14 @@
     stats_ref[...] = jnp.broadcast_to(rows[None], stats_ref.shape)
 
 
-def scales(stats_ref):
-    total = jnp.sum(stats_ref[...], axis=0)
+def scales(here_ref, there_ref):
+    total = jnp.sum(here_ref[...], axis=0) + jnp.sum(there_ref[...], axis=0)
     rinv = lax.rsqrt(total[0:1] / C + 1e-06)
     return down(rinv, BLOCK), down(rinv * rinv * rinv * total[1:2] / C, BLOCK)
 
 
-def filter_kernel(dft_ref, seg_ref, stats_ref, conv_ref, spec_ref, rest_ref, q_ref, g_ref, gain_ref, chunk_ref, head_ref):
-    rinv, slope = scales(stats_ref)
+def filter_kernel(dft_ref, seg_ref, here_ref, there_ref, conv_ref, spec_ref, rest_ref, q_ref, g_ref, gain_ref, chunk_ref, head_ref):
+    rinv, slope = scales(here_ref, there_ref)
     seg = seg_ref[...]
     first = down(first_doc(seg), BLOCK).astype(jnp.bfloat16)
     is_end = lax.broadcasted_iota(jnp.int32, (ROWS, BLOCK), 0) == ROWS - 1
@@ -202,9 +218,9 @@
                 chunk_ref[group, block, 8] = gain_both[:, lanes]
 
 
-def out_kernel(q_hbm, g_hbm, k_hbm, v_hbm, dft_ref, seg_ref, stats_ref, conv_ref, taps_ref, gain_ref, layer_ref, qg_ref, dprod_ref, k_ref, v_ref, q_ref, g_ref, sems):
+def out_kernel(q_hbm, g_hbm, k_hbm, v_hbm, dft_ref, seg_ref, here_ref, there_ref, conv_ref, taps_ref, gain_ref, layer_ref, qg_ref, dprod_ref, k_ref, v_ref, q_ref, g_ref, sems):
     copies = fetch([(q_hbm, q_ref), (g_hbm, g_ref), (k_hbm, k_ref), (v_hbm, v_ref)], sems)
-    rinv, slope = scales(stats_ref)
+    rinv, slope = scales(here_ref, there_ref)
     seg = seg_ref[...]
     in_last = down(last_doc(seg), BLOCK)
     in_first = down(first_doc(seg), BLOCK).astype(jnp.bfloat16)
@@ -240,13 +256,17 @@
         vg_ref[:, at] = (dprod * k_ref[:, at].astype(jnp.float32)).astype(jnp.bfloat16)
 
 
-def total_kernel(parts_ref, mine_ref):
+def total_kernel(parts_ref, mine_hbm, mine_ref, sems):
     total = jnp.sum(parts_ref[...].astype(jnp.float32), axis=0)
     gain = total[8, 0:1] + total[8, 1:2]
     gain_high = gain.astype(jnp.bfloat16)
     gain_low = (gain - gain_high.astype(jnp.float32)).astype(jnp.bfloat16)
     mine = jnp.concatenate([total[:8].astype(jnp.bfloat16), jnp.concatenate([gain_high, gain_low], axis=0)[None]], axis=0)
     mine_ref[...] = jnp.broadcast_to(mine[None], mine_ref.shape)
+    some = mine_ref.shape[0]
+    copies = fetch([(mine_ref, mine_hbm.at[pl.ds(i, some)]) for i in range(0, parts_ref.shape[0], some)], sems)
+    for copy in copies:
+        copy.wait()
 
 
 def gather_kernel(full_ref, filt_ref, gain_ref):
@@ -260,7 +280,7 @@
         gain_ref[:, lanes] = gain[0:1] + gain[1:2]
 
 
-def call(kernel, name, outs, flops, hbm, vmem, scratch=(), pinned=True):
+def call(kernel, name, outs, flops, hbm, vmem, scratch=(), pinned=True, sent=0):
     hbm = [pltpu.with_memory_space_constraint(a, pltpu.HBM) for a in hbm]
     args = (*hbm, *vmem)
     moved = sum(a.size * a.dtype.itemsize for a in args)
@@ -269,7 +289,7 @@
     return pl.pallas_call(
         kernel,
         in_specs=[pl.BlockSpec(memory_space=pltpu.HBM)] * len(hbm) + [here] * len(vmem),
-        out_specs=[here] * len(outs),
+        out_specs=[pl.BlockSpec(memory_space=pltpu.HBM)] * sent + [here] * (len(outs) - sent),
         out_shape=[space(shape, dtype) for shape, dtype in outs],
         scratch_shapes=scratch,
         compiler_params=pltpu.CompilerParams(vmem_limit_bytes=32 * 1024 * 1024),
@@ -278,15 +298,9 @@
     )(*args)
 
 
-def shifted(value, axis, steps):
-    count = lax.axis_size(axis)
-    first, last = (max(0, -steps), min(count, count - steps))
-    return lax.ppermute(value, axis, [(source, source + steps) for source in range(first, last)])
-
-
 def local(q_act, k_act, v_act, filt, gain, segments, grad_out):
     width = q_act.shape[1]
-    n_ctx, n_hid = lax.axis_size("ctx"), lax.axis_size("hid")
+    n_ctx, n_x = lax.axis_size("ctx"), lax.axis_size("x")
     dft = jnp.asarray(transforms())
     seg = segments.reshape(1, ROWS)
     gain_row = gain.reshape(1, width)
@@ -296,12 +310,17 @@
     unit = 2**27
 
     row = ((1, width), jnp.float32)
-    sems = pltpu.SemaphoreType.DMA((1 + 2 * (width // BLOCK),))
+    sems = pltpu.SemaphoreType.DMA((1 + 2 * (width // PART),))
     mine = pltpu.VMEM((ROWS, width), jnp.bfloat16)
+    (far,) = call(
+        far_kernel, "far_message", [act], 2**18, (seg, k_act, v_act), (), [pltpu.VMEM((1, ROWS), jnp.int32), mine, mine, sems]
+    )
     seg, prod, message = call(
         message_kernel, "message", [((1, ROWS), jnp.int32), act, act], 2**18, (seg, k_act, v_act), (), [mine, mine, sems]
     )
-    halo = shifted(message, "ctx", 1)
+    edges = [(source, source + 1) for source in range(n_ctx - 1)]
+    far_halo = lax.ppermute(far, "ctx", [edge for edge in edges if edge[1] % RUN == 0])
+    halo = lax.ppermute(message, "ctx", [edge for edge in edges if edge[1] % RUN])
     dft, q_here, g_here, gain_here, taps, all_spec, rest_spec, own_conv = call(
         own_kernel,
         "own_conv",
@@ -314,12 +333,13 @@
     conv, all_spec, stats = call(
         halo_kernel,
         "halo_conv",
-        [wide, spec, ((n_hid, 2, ROWS), jnp.float32)],
+        [wide, spec, ((n_x, 2, ROWS), jnp.float32)],
         3 * unit,
         (),
-        (dft, seg, halo, taps, all_spec, own_conv, q_here, g_here, gain_here),
-    )
-    stats = lax.all_to_all(stats, "hid", 0, 0, tiled=True)
+        (dft, seg, halo, far_halo, taps, all_spec, own_conv, q_here, g_here, gain_here),
+    )
+    here = lax.all_to_all(stats, "x", 0, 0, tiled=True)
+    there = lax.ppermute(here, "z_hi", [(0, 1), (1, 0)])
 
     groups = (8, width // ROWS, 9, 2, ROWS)
     chunks, head = call(
@@ -328,20 +348,21 @@
         [(groups, jnp.bfloat16), act],
         5 * unit,
         (),
-        (dft, seg, stats, conv, all_spec, rest_spec, q_here, g_here, gain_here),
+        (dft, seg, here, there, conv, all_spec, rest_spec, q_here, g_here, gain_here),
     )
     parts = lax.all_to_all(chunks.reshape(n_ctx, 9, 2, ROWS), "ctx", 0, 0, tiled=True)
     parts, head = lax.optimization_barrier((parts, head))
-    (total,) = call(total_kernel, "total", [(parts.shape, parts.dtype)], 2**18, (), (parts,))
+    some = [pltpu.VMEM((n_ctx // COPIES, 9, 2, ROWS), jnp.bfloat16), pltpu.SemaphoreType.DMA((COPIES,))]
+    (total,) = call(total_kernel, "total", [(parts.shape, parts.dtype)], 2**18, (), (parts,), some, False, 1)
     full = lax.all_to_all(total, "ctx", 0, 0, tiled=True)
-    tail = shifted(head, "ctx", -1)
+    tail = lax.ppermute(head, "ctx", [(target, source) for source, target in edges])
     layer_out, q_grad, own_dprod, k_here, v_here = call(
         out_kernel,
         "out_grads",
         [act, act, wide, act, act],
         6 * unit,
         (q_act, grad_out, k_act, v_act),
-        (dft, seg, stats, conv, taps, gain_here),
+        (dft, seg, here, there, conv, taps, gain_here),
         [mine, mine, pltpu.SemaphoreType.DMA((4,))],
         False,
     )
@@ -355,21 +376,9 @@
 
 
 def solution(mesh):
-    in_specs = (
-        P("ctx", "hid"),
-        P("ctx", "hid"),
-        P("ctx", "hid"),
-        P(None, "hid"),
-        P("hid"),
-        P("ctx"),
-        P("ctx", "hid"),
-    )
-    out_specs = (
-        P("ctx", "hid"),
-        P("ctx", "hid"),
-        P("ctx", "hid"),
-        P("ctx", "hid"),
-        P(None, "hid"),
-        P("hid"),
-    )
-    return jax.shard_map(local, mesh=mesh, in_specs=in_specs, out_specs=out_specs, check_vma=False)
+    n_ctx, n_hid = mesh.shape["ctx"], mesh.shape["hid"]
+    split = Mesh(mesh.devices.reshape(n_ctx, n_hid // 2, 2), ("ctx", *HID))
+    tile, by_hid = P("ctx", HID), P(None, HID)
+    in_specs = (tile, tile, tile, by_hid, P(HID), P("ctx"), tile)
+    out_specs = (tile, tile, tile, tile, by_hid, P(HID))
+    return jax.shard_map(local, mesh=split, in_specs=in_specs, out_specs=out_specs, check_vma=False)

time: 81.9 us -> 80.2 us (0.979)
  blocking collectives: 47.2 us -> 34.4 us
  starting transfers between devices: 12.9 us -> 23.3 us
  waiting for transfers between devices: 6.02 us -> 8.27 us
  Pallas kernels: 14.7 us -> 13.2 us
    all_to_all x1, blocking collectives: 19.8 us -> 7.47 us  [local(): here = lax.all_to_all(stats, 'x', 0, 0, tiled=True)]
    ppermute x2 -> x4, starting transfers between devices: 7.75 us -> 18.2 us  [the longest x1 9.73 us: local(): there = lax.ppermute(here, 'z_hi', [(0, 1), (1, 0)])]
    ppermute x2 -> x4, waiting for transfers between devices: 6.01 us -> 8.03 us  [the longest x1 5.77 us: local(): lax.ppermute(head, 'ctx', [(target, source) for source, target in edges])]
    pallas_call x8 -> x9, Pallas kernels: 14.7 us -> 13.2 us  [call(): pl.pallas_call(kernel, in_specs=[pl.BlockSpec(memory_space=pltpu.HBM)] *...]
  transfers between devices with their start and end apart: 3 -> 5, of which waited for: 2 -> 4; matrix products, arithmetic and copies ran while one was open for 0% -> 0% of each run, Pallas kernels for 11% -> 11%
where the time goes in v4:
time: 80.2 us; the launch traced here: 79.9 us
  blocking collectives  34.4 us (43%)
  starting transfers between devices  23.3 us (29%)
  Pallas kernels  13.2 us (16%)
  waiting for transfers between devices  8.27 us (10%)
    all_to_all x1, blocking collectives, local(): lax.all_to_all(chunks.reshape(n_ctx, 9, 2, ROWS), 'ctx', 0, 0, tiled=True)  26.9 us
    pallas_call x9, Pallas kernels, call(): pl.pallas_call(kernel, in_specs=[pl.BlockSpec(memory_space=pltpu.HBM)] *...  13.2 us
    ppermute x1, starting transfers between devices, local(): there = lax.ppermute(here, 'z_hi', [(0, 1), (1, 0)])  9.73 us
    all_to_all x1, blocking collectives, local(): here = lax.all_to_all(stats, 'x', 0, 0, tiled=True)  7.47 us
    ppermute x1, waiting for transfers between devices, local(): lax.ppermute(head, 'ctx', [(target, source) for source, target in edges])  5.77 us
    ppermute x1, starting transfers between devices, local(): lax.ppermute(message, 'ctx', [edge for edge in edges if edge[1] % RUN])  5.39 us
    all_to_all x1, starting transfers between devices, local(): full = lax.all_to_all(total, 'ctx', 0, 0, tiled=True)  5.16 us
    ppermute x1, starting transfers between devices, local(): lax.ppermute(head, 'ctx', [(target, source) for source, target in edges])  2.36 us
  transfers between devices with their start and end apart: 5, of which 4 were waited for; matrix products, arithmetic and copies ran while one was open for 0% of the time, Pallas kernels for 11%

profile of v4, /device:TPU:1, one launch (start us, length us, event | category | flops | bytes accessed | tf_op | source)
XLA Modules:
  0.0 79.9 jit_solution(7315553059302824926)
XLA Ops:
  0.6 0.1 far_message.1
  0.7 0.7 collective-permute-start.1
  1.4 1.2 %message.1 = (s32[1,128]{1,0:T(1,128)S(1)}, bf16[128,1024]{1,0:T(8,128)(2,1)S(1)}, bf16[128,1024]{1,0:T(8,128)(2,1)S(1)}) custom-call(s32[1,128]{1,0:T(1,128)} %bitcast.8, bf16[128,1024]{1,0:T(8,128)(2,1)} %k_hbm.5, bf16[128,1024]{1,0:T(8,128)(2,1)} %v_hbm.5), custom_call_target="tpu_custom_call" | custom-call | flops 262144 | bytes 524800 | tf_op jit(solution)/shard_map/message/pallas_call | solution.py:289
  2.6 5.4 %collective-permute-start = (bf16[128,1024]{1,0:T(8,128)(2,1)S(1)}, bf16[128,1024]{1,0:T(8,128)(2,1)S(1)}, u32[]{:S(2)}, u32[]{:S(2)}) collective-permute-start(bf16[128,1024]{1,0:T(8,128)(2,1)S(1)} %get-tuple-element.36), channel_id=1, source_target_pairs={{0,8},{8,16},{16,24},{24,32},{32,40},{40,48},{48,56},{64,72},{72,8... | collective-permute-start | bytes 786440 | tf_op jit(solution)/shard_map/ppermute | solution.py:323
  8.0 2.7 %own_conv.1 = (bf16[4,256,256]{2,1,0:T(8,128)(2,1)S(1)}, bf16[128,1024]{1,0:T(8,128)(2,1)S(1)}, bf16[128,1024]{1,0:T(8,128)(2,1)S(1)}, f32[1,1024]{1,0:T(1,128)S...) custom-call(bf16[4,256,256]{2,1,0:T(8,128)(2,1)} %constant.2.clone.d, ...), custom_call_target="tpu_custom_call" | custom-call | flops 1073741824 | bytes 1839616 | tf_op jit(solution)/shard_map/own_conv/pallas_call | solution.py:289
  10.7 0.0 collective-permute-done.1.far_ref
  10.7 1.1 %collective-permute-done.near_ref = bf16[128,1024]{1,0:T(8,128)(2,1)S(1)} collective-permute-done((bf16[128,1024]{1,0:T(8,128)(2,1)S(1)}, bf16[128,1024]{1,0:T(8,128)(2,1)S(1)}, u32[]{:S(2)}, u32[]{:S(2)}) %collective-permute-start) | collective-permute-done | bytes 262176 | tf_op jit(solution)/shard_map/ppermute | solution.py:323
  11.8 1.0 %halo_conv.1 = (f32[128,1024]{1,0:T(8,128)S(1)}, f32[256,1024]{1,0:T(8,128)S(1)}, f32[4,2,128]{2,1,0:T(2,128)S(1)}) custom-call(bf16[4,256,256]{2,1,0:T(8,128)(2,1)S(1)} %get-tuple-element.35.dft_ref, s32[1,128]{1,0:T(1,128)S(1)} %get-tuple-element.33.seg_ref, bf16[128,1024]{1,0:T(8,128)(2,1)S(1)} %collective-permute-done.near_ref, ...), custom_call_target="tpu_custom_call" | custom-call | flops 402653184 | bytes 4198912 | tf_op jit(solution)/shard_map/halo_conv/pallas_call | solution.py:289
  12.8 7.5 %all_to_all.15.here_ref = f32[4,2,128]{2,1,0:T(2,128)S(1)} all-to-all(f32[4,2,128]{2,1,0:T(2,128)S(1)} %get-tuple-element.43), channel_id=1, replica_groups=mesh['ctx'=64,'x'=4,'z_hi'=2] {'x'}, dimensions={0} | all-to-all | bytes 8192 | tf_op jit(solution)/shard_map/all_to_all | solution.py:341
  20.2 9.7 %collective-permute-start.2 = (f32[4,2,128]{2,1,0:T(2,128)S(1)}, f32[4,2,128]{2,1,0:T(2,128)S(1)}, u32[]{:S(2)}, u32[]{:S(2)}) collective-permute-start(f32[4,2,128]{2,1,0:T(2,128)S(1)} %all_to_all.15.here_ref), channel_id=1, source_target_pairs={{0,1},{1,0},{2,3},{3,2},{4,5},{5,4},{6,7},{7,6},{8,9},{9,8},{10,11... | collective-permute-start | bytes 12296 | tf_op jit(solution)/shard_map/ppermute | solution.py:342
  30.0 1.2 %collective-permute-done.2.there_ref = f32[4,2,128]{2,1,0:T(2,128)S(1)} collective-permute-done((f32[4,2,128]{2,1,0:T(2,128)S(1)}, f32[4,2,128]{2,1,0:T(2,128)S(1)}, u32[]{:S(2)}, u32[]{:S(2)}) %collective-permute-start.2) | collective-permute-done | bytes 4128 | tf_op jit(solution)/shard_map/ppermute | solution.py:342
  31.1 1.4 %filter_grad.1 = (bf16[8,8,9,2,128]{4,3,2,1,0:T(2,128)(2,1)S(1)}, bf16[128,1024]{1,0:T(8,128)(2,1)S(1)}) custom-call(bf16[4,256,256]{2,1,0:T(8,128)(2,1)S(1)} %get-tuple-element.35.dft_ref, s32[1,128]{1,0:T(1,128)S(1)} %get-tuple-element.33.seg_ref, f32[4,2,128]{2,1,0:T(2,128)S(1)} %all_to_all.15.here_ref, ...), custom_call_target="tpu_custom_call" | custom-call | flops 671088640 | bytes 3682816 | tf_op jit(solution)/shard_map/filter_grad/pallas_call | solution.py:289
  32.5 26.9 %all_to_all.16.parts_ref = bf16[64,9,2,128]{3,2,1,0:T(2,128)(2,1)S(1)} all-to-all(bf16[64,9,2,128]{3,2,1,0:T(2,128)(2,1)S(1)} %bitcast.6), channel_id=1, replica_groups=mesh['ctx'=64,'x'=4,'z_hi'=2] {'ctx'}, dimensions={0} | all-to-all | bytes 589824 | tf_op jit(solution)/shard_map/all_to_all | solution.py:353
  59.4 1.0 %total.1 = bf16[64,9,2,128]{3,2,1,0:T(2,128)(2,1)} custom-call(bf16[64,9,2,128]{3,2,1,0:T(2,128)(2,1)S(1)} %all_to_all.16.parts_ref), custom_call_target="tpu_custom_call" | custom-call | flops 262144 | bytes 294912 | tf_op jit(solution)/shard_map/total/pallas_call | solution.py:289
  60.4 5.2 %all-to-all-start.2 = ((bf16[64,9,2,128]{3,2,1,0:T(2,128)(2,1)}), bf16[64,9,2,128]{3,2,1,0:T(2,128)(2,1)S(1)}, u32[]{:S(2)}, u32[]{:S(2)}) async-start(bf16[64,9,2,128]{3,2,1,0:T(2,128)(2,1)} %total.1), calls=%async_computation.2 | async-start | bytes 589824 | tf_op jit(solution)/shard_map/all_to_all | solution.py:357
  65.6 2.4 %collective-permute-start.3 = (bf16[128,1024]{1,0:T(8,128)(2,1)S(1)}, bf16[128,1024]{1,0:T(8,128)(2,1)S(1)}, u32[]{:S(2)}, u32[]{:S(2)}) collective-permute-start(bf16[128,1024]{1,0:T(8,128)(2,1)S(1)} %get-tuple-element.52), channel_id=1, source_target_pairs={{8,0},{16,8},{24,16},{32,24},{40,32},{48,40},{56,48},{64,56},{72,6... | collective-permute-start | bytes 786440 | tf_op jit(solution)/shard_map/ppermute | solution.py:358
  68.0 3.2 %out_grads.1 = (bf16[128,1024]{1,0:T(8,128)(2,1)}, bf16[128,1024]{1,0:T(8,128)(2,1)}, f32[128,1024]{1,0:T(8,128)S(1)}, bf16[128,1024]{1,0:T(8,128)(2,1)S(1)}, bf16[128,1024]{1,0:T(8,128)(2,1)S(1)}) custom-call(bf16[128,1024]{1,0:T(8,128)(2,1)} %q_hbm.3, bf16[128,1024]{1,0:T(8,128)(2,1)} %g_hbm.3, bf16[128,1024]{1,0:T(8,128)(2,1)} %k_hbm.5, ...), custom_call_target="tpu_custom_call" | custom-call | flops 805306368 | bytes 3158528 | tf_op jit(solution)/shard_map/out_grads/pallas_call | solution.py:289
  71.2 5.8 %collective-permute-done.3.tail_ref = bf16[128,1024]{1,0:T(8,128)(2,1)S(1)} collective-permute-done((bf16[128,1024]{1,0:T(8,128)(2,1)S(1)}, bf16[128,1024]{1,0:T(8,128)(2,1)S(1)}, u32[]{:S(2)}, u32[]{:S(2)}) %collective-permute-start.3) | collective-permute-done | bytes 262176 | tf_op jit(solution)/shard_map/ppermute | solution.py:358
  77.0 1.6 %input_grads.1 = (bf16[128,1024]{1,0:T(8,128)(2,1)}, bf16[128,1024]{1,0:T(8,128)(2,1)}) custom-call(bf16[4,256,256]{2,1,0:T(8,128)(2,1)S(1)} %get-tuple-element.35.dft_ref, s32[1,128]{1,0:T(1,128)S(1)} %get-tuple-element.33.seg_ref, f32[128,1024]{1,0:T(8,128)S(1)} %get-tuple-element.47.dprod_ref, bf16[128,1024]{1,0:T(8,128)(2,1)S(1)} %collective-permute-done.3.tail_ref, ...), custom_call_target="tpu_custom_call" | custom-call | flops 402653184 | bytes 2884096 | tf_op jit(solution)/shard_map/input_grads/pallas_call | solution.py:289
  78.6 0.2 all-to-all-done.2
  78.8 1.0 %gather.1 = (f32[128,1024]{1,0:T(8,128)}, f32[1,1024]{1,0:T(1,128)}) custom-call(bf16[8,8,9,2,128]{4,3,2,1,0:T(2,128)(2,1)S(1)} %bitcast.5), custom_call_target="tpu_custom_call" | custom-call | flops 262144 | bytes 294912 | tf_op jit(solution)/shard_map/gather/pallas_call | solution.py:289
Async XLA Ops:
  0.7 10.0 %collective-permute-start.1 = (bf16[128,1024]{1,0:T(8,128)(2,1)S(1)}, bf16[128,1024]{1,0:T(8,128)(2,1)S(1)}, u32[]{:S(2)}, u32[]{:S(2)}) collective-permute-start(bf16[128,1024]{1,0:T(8,128)(2,1)S(1)} %far_message.1), channel_id=1, source_target_pairs={{56,64},{120,128},{184,192},{248,256},{312,320},{376,384},{440,448... | collective-permute-start | bytes 786440 | tf_op jit(solution)/shard_map/ppermute | solution.py:322
  2.6 9.2 %collective-permute-start = (bf16[128,1024]{1,0:T(8,128)(2,1)S(1)}, bf16[128,1024]{1,0:T(8,128)(2,1)S(1)}, u32[]{:S(2)}, u32[]{:S(2)}) collective-permute-start(bf16[128,1024]{1,0:T(8,128)(2,1)S(1)} %get-tuple-element.36), channel_id=1, source_target_pairs={{0,8},{8,16},{16,24},{24,32},{32,40},{40,48},{48,56},{64,72},{72,8... | collective-permute-start | bytes 786440 | tf_op jit(solution)/shard_map/ppermute | solution.py:323
  20.2 10.9 %collective-permute-start.2 = (f32[4,2,128]{2,1,0:T(2,128)S(1)}, f32[4,2,128]{2,1,0:T(2,128)S(1)}, u32[]{:S(2)}, u32[]{:S(2)}) collective-permute-start(f32[4,2,128]{2,1,0:T(2,128)S(1)} %all_to_all.15.here_ref), channel_id=1, source_target_pairs={{0,1},{1,0},{2,3},{3,2},{4,5},{5,4},{6,7},{7,6},{8,9},{9,8},{10,11... | collective-permute-start | bytes 12296 | tf_op jit(solution)/shard_map/ppermute | solution.py:342
  60.4 18.4 %all-to-all-start.2 = ((bf16[64,9,2,128]{3,2,1,0:T(2,128)(2,1)}), bf16[64,9,2,128]{3,2,1,0:T(2,128)(2,1)S(1)}, u32[]{:S(2)}, u32[]{:S(2)}) async-start(bf16[64,9,2,128]{3,2,1,0:T(2,128)(2,1)} %total.1), calls=%async_computation.2 | async-start | bytes 589824 | tf_op jit(solution)/shard_map/all_to_all | solution.py:357
  65.6 11.4 %collective-permute-start.3 = (bf16[128,1024]{1,0:T(8,128)(2,1)S(1)}, bf16[128,1024]{1,0:T(8,128)(2,1)S(1)}, u32[]{:S(2)}, u32[]{:S(2)}) collective-permute-start(bf16[128,1024]{1,0:T(8,128)(2,1)S(1)} %get-tuple-element.52), channel_id=1, source_target_pairs={{8,0},{16,8},{24,16},{32,24},{40,32},{48,40},{56,48},{64,56},{72,6... | collective-permute-start | bytes 786440 | tf_op jit(solution)/shard_map/ppermute | solution.py:358

commit v5 on v4

--- a/solution.py
+++ b/solution.py
@@ -159,7 +159,7 @@
         copy.wait()
 
 
-def halo_kernel(dft_ref, seg_ref, near_ref, far_ref, taps_ref, all_ref, own_conv_ref, q_ref, g_ref, gain_ref, conv_ref, spec_ref, stats_ref):
+def halo_kernel(dft_ref, seg_ref, near_ref, far_ref, taps_ref, own_conv_ref, q_ref, g_ref, gain_ref, conv_ref, stats_ref):
     seg = seg_ref[...]
     in_first = down(first_doc(seg), BLOCK)
     mark = parity(seg[:, :1])
@@ -169,7 +169,6 @@
         halo = near_ref[:, at] + far_ref[:, at]
         joined = (halo[0:1].astype(jnp.float32) == mark).astype(jnp.float32)
         halo_spec = forward(left, halo) * joined
-        spec_ref[:, at] = all_ref[:, at] + halo_spec
         conv = own_conv_ref[:, at] + in_first * backward(back, times(halo_spec, taps_ref[:, at]))
         conv_ref[:, at] = conv
         y = q_ref[:, at].astype(jnp.float32) * conv
@@ -179,14 +178,23 @@
     stats_ref[...] = jnp.broadcast_to(rows[None], stats_ref.shape)
 
 
-def scales(here_ref, there_ref):
-    total = jnp.sum(here_ref[...], axis=0) + jnp.sum(there_ref[...], axis=0)
+def spectrum_kernel(dft_ref, seg_ref, near_ref, far_ref, all_ref, spec_ref):
+    mark = parity(seg_ref[:, :1])
+    left = dft_ref[2]
+    for at in blocks(all_ref.shape[1]):
+        halo = near_ref[:, at] + far_ref[:, at]
+        joined = (halo[0:1].astype(jnp.float32) == mark).astype(jnp.float32)
+        spec_ref[:, at] = all_ref[:, at] + forward(left, halo) * joined
+
+
+def scales(stats_ref):
+    total = jnp.sum(stats_ref[...], axis=0)
     rinv = lax.rsqrt(total[0:1] / C + 1e-06)
     return down(rinv, BLOCK), down(rinv * rinv * rinv * total[1:2] / C, BLOCK)
 
 
-def filter_kernel(dft_ref, seg_ref, here_ref, there_ref, conv_ref, spec_ref, rest_ref, q_ref, g_ref, gain_ref, chunk_ref, head_ref):
-    rinv, slope = scales(here_ref, there_ref)
+def filter_kernel(dft_ref, seg_ref, stats_ref, conv_ref, spec_ref, rest_ref, q_ref, g_ref, gain_ref, chunk_ref, head_ref):
+    rinv, slope = scales(stats_ref)
     seg = seg_ref[...]
     first = down(first_doc(seg), BLOCK).astype(jnp.bfloat16)
     is_end = lax.broadcasted_iota(jnp.int32, (ROWS, BLOCK), 0) == ROWS - 1
@@ -218,9 +226,9 @@
                 chunk_ref[group, block, 8] = gain_both[:, lanes]
 
 
-def out_kernel(q_hbm, g_hbm, k_hbm, v_hbm, dft_ref, seg_ref, here_ref, there_ref, conv_ref, taps_ref, gain_ref, layer_ref, qg_ref, dprod_ref, k_ref, v_ref, q_ref, g_ref, sems):
+def out_kernel(q_hbm, g_hbm, k_hbm, v_hbm, dft_ref, seg_ref, stats_ref, conv_ref, taps_ref, gain_ref, layer_ref, qg_ref, dprod_ref, k_ref, v_ref, q_ref, g_ref, sems):
     copies = fetch([(q_hbm, q_ref), (g_hbm, g_ref), (k_hbm, k_ref), (v_hbm, v_ref)], sems)
-    rinv, slope = scales(here_ref, there_ref)
+    rinv, slope = scales(stats_ref)
     seg = seg_ref[...]
     in_last = down(last_doc(seg), BLOCK)
     in_first = down(first_doc(seg), BLOCK).astype(jnp.bfloat16)
@@ -330,16 +338,18 @@
         (seg, prod),
         [pltpu.VMEM(filt.shape, filt.dtype), pltpu.SemaphoreType.DMA((5,))],
     )
-    conv, all_spec, stats = call(
+    conv, stats = call(
         halo_kernel,
         "halo_conv",
-        [wide, spec, ((n_x, 2, ROWS), jnp.float32)],
+        [wide, ((n_x, 2, ROWS), jnp.float32)],
         3 * unit,
         (),
-        (dft, seg, halo, far_halo, taps, all_spec, own_conv, q_here, g_here, gain_here),
-    )
-    here = lax.all_to_all(stats, "x", 0, 0, tiled=True)
-    there = lax.ppermute(here, "z_hi", [(0, 1), (1, 0)])
+        (dft, seg, halo, far_halo, taps, own_conv, q_here, g_here, gain_here),
+    )
+    all_spec = call(spectrum_kernel, "spectrum", [spec], unit, (), (dft, seg, halo, far_halo, all_spec))[0]
+    stats = stats + lax.ppermute(stats, "z_hi", [(0, 1), (1, 0)])
+    stats, all_spec = lax.optimization_barrier((stats, all_spec))
+    stats = lax.all_to_all(stats, "x", 0, 0, tiled=True)
 
     groups = (8, width // ROWS, 9, 2, ROWS)
     chunks, head = call(
@@ -348,7 +358,7 @@
         [(groups, jnp.bfloat16), act],
         5 * unit,
         (),
-        (dft, seg, here, there, conv, all_spec, rest_spec, q_here, g_here, gain_here),
+        (dft, seg, stats, conv, all_spec, rest_spec, q_here, g_here, gain_here),
     )
     parts = lax.all_to_all(chunks.reshape(n_ctx, 9, 2, ROWS), "ctx", 0, 0, tiled=True)
     parts, head = lax.optimization_barrier((parts, head))
@@ -362,7 +372,7 @@
         [act, act, wide, act, act],
         6 * unit,
         (q_act, grad_out, k_act, v_act),
-        (dft, seg, here, there, conv, taps, gain_here),
+        (dft, seg, stats, conv, taps, gain_here),
         [mine, mine, pltpu.SemaphoreType.DMA((4,))],
         False,
     )

time: 80.2 us -> 80.3 us (level)
    pallas_call x9 -> x10, Pallas kernels: 13.2 us -> 13.5 us  [call(): pl.pallas_call(kernel, in_specs=[pl.BlockSpec(memory_space=pltpu.HBM)] *...]
where the time goes in v5:
time: 80.3 us; the launch traced here: 79.9 us
  blocking collectives  35.1 us (44%)
  starting transfers between devices  22.8 us (28%)
  Pallas kernels  13.5 us (17%)
  waiting for transfers between devices  7.72 us (10%)
    all_to_all x1, blocking collectives, local(): lax.all_to_all(chunks.reshape(n_ctx, 9, 2, ROWS), 'ctx', 0, 0, tiled=True)  26.9 us
    pallas_call x10, Pallas kernels, call(): pl.pallas_call(kernel, in_specs=[pl.BlockSpec(memory_space=pltpu.HBM)] *...  13.5 us
    ppermute x1, starting transfers between devices, local(): stats = stats + lax.ppermute(stats, 'z_hi', [(0, 1), (1, 0)])  9.25 us
    all_to_all x1, blocking collectives, local(): stats = lax.all_to_all(stats, 'x', 0, 0, tiled=True)  8.15 us
    ppermute x1, waiting for transfers between devices, local(): lax.ppermute(head, 'ctx', [(target, source) for source, target in edges])  5.77 us
    ppermute x1, starting transfers between devices, local(): lax.ppermute(message, 'ctx', [edge for edge in edges if edge[1] % RUN])  5.39 us
    all_to_all x1, starting transfers between devices, local(): full = lax.all_to_all(total, 'ctx', 0, 0, tiled=True)  5.16 us
    ppermute x1, starting transfers between devices, local(): lax.ppermute(head, 'ctx', [(target, source) for source, target in edges])  2.36 us
  transfers between devices with their start and end apart: 5, of which 4 were waited for; matrix products, arithmetic and copies ran while one was open for 0% of the time, Pallas kernels for 11%

profile of v5, /device:TPU:1, one launch (start us, length us, event | category | flops | bytes accessed | tf_op | source)
XLA Modules:
  0.0 79.9 jit_solution(1516084979392587306)
XLA Ops:
  0.6 0.1 far_message.1
  0.7 0.7 collective-permute-start.1
  1.4 1.2 %message.1 = (s32[1,128]{1,0:T(1,128)S(1)}, bf16[128,1024]{1,0:T(8,128)(2,1)S(1)}, bf16[128,1024]{1,0:T(8,128)(2,1)S(1)}) custom-call(s32[1,128]{1,0:T(1,128)} %bitcast.8, bf16[128,1024]{1,0:T(8,128)(2,1)} %k_hbm.5, bf16[128,1024]{1,0:T(8,128)(2,1)} %v_hbm.5), custom_call_target="tpu_custom_call" | custom-call | flops 262144 | bytes 524800 | tf_op jit(solution)/shard_map/message/pallas_call | solution.py:297
  2.6 5.4 %collective-permute-start = (bf16[128,1024]{1,0:T(8,128)(2,1)S(1)}, bf16[128,1024]{1,0:T(8,128)(2,1)S(1)}, u32[]{:S(2)}, u32[]{:S(2)}) collective-permute-start(bf16[128,1024]{1,0:T(8,128)(2,1)S(1)} %get-tuple-element.37), channel_id=1, source_target_pairs={{0,8},{8,16},{16,24},{24,32},{32,40},{40,48},{48,56},{64,72},{72,8... | collective-permute-start | bytes 786440 | tf_op jit(solution)/shard_map/ppermute | solution.py:331
  8.0 2.7 %own_conv.1 = (bf16[4,256,256]{2,1,0:T(8,128)(2,1)S(1)}, bf16[128,1024]{1,0:T(8,128)(2,1)S(1)}, bf16[128,1024]{1,0:T(8,128)(2,1)S(1)}, f32[1,1024]{1,0:T(1,128)S...) custom-call(bf16[4,256,256]{2,1,0:T(8,128)(2,1)} %constant.2.clone.d, ...), custom_call_target="tpu_custom_call" | custom-call | flops 1073741824 | bytes 1839616 | tf_op jit(solution)/shard_map/own_conv/pallas_call | solution.py:297
  10.7 0.0 collective-permute-done.1.far_ref
  10.8 1.0 %collective-permute-done.near_ref = bf16[128,1024]{1,0:T(8,128)(2,1)S(1)} collective-permute-done((bf16[128,1024]{1,0:T(8,128)(2,1)S(1)}, bf16[128,1024]{1,0:T(8,128)(2,1)S(1)}, u32[]{:S(2)}, u32[]{:S(2)}) %collective-permute-start) | collective-permute-done | bytes 262176 | tf_op jit(solution)/shard_map/ppermute | solution.py:331
  11.8 0.9 %halo_conv.1 = (f32[128,1024]{1,0:T(8,128)S(1)}, f32[4,2,128]{2,1,0:T(2,128)S(1)}) custom-call(bf16[4,256,256]{2,1,0:T(8,128)(2,1)S(1)} %get-tuple-element.36.dft_ref, s32[1,128]{1,0:T(1,128)S(1)} %get-tuple-element.34.seg_ref, bf16[128,1024]{1,0:T(8,128)(2,1)S(1)} %collective-permute-done.near_ref, bf16[128,1024]{1,0:T(8,128)(2,1)S(1)} %collective-permute-done.1.far_ref, ...), custom_call_target="tpu_custom_call" | custom-call | flops 402653184 | bytes 3150336 | tf_op jit(solution)/shard_map/halo_conv/pallas_call | solution.py:297
  12.7 9.2 %collective-permute-start.2 = (f32[4,2,128]{2,1,0:T(2,128)S(1)}, f32[4,2,128]{2,1,0:T(2,128)S(1)}, u32[]{:S(2)}, u32[]{:S(2)}) collective-permute-start(f32[4,2,128]{2,1,0:T(2,128)S(1)} %get-tuple-element.43), channel_id=1, source_target_pairs={{0,1},{1,0},{2,3},{3,2},{4,5},{5,4},{6,7},{7,6},{8,9},{9,8},{10,11... | collective-permute-start | bytes 12296 | tf_op jit(solution)/shard_map/ppermute | solution.py:350
  22.0 0.3 spectrum.1.spec_ref
  22.3 0.7 collective-permute-done.2
  23.0 8.1 %all_to_all.15.stats_ref = f32[4,2,128]{2,1,0:T(2,128)S(1)} all-to-all(f32[4,2,128]{2,1,0:T(2,128)S(1)} %add.3), channel_id=1, replica_groups=mesh['ctx'=64,'x'=4,'z_hi'=2] {'x'}, dimensions={0} | all-to-all | bytes 8192 | tf_op jit(solution)/shard_map/all_to_all | solution.py:352
  31.1 1.4 %filter_grad.1 = (bf16[8,8,9,2,128]{4,3,2,1,0:T(2,128)(2,1)S(1)}, bf16[128,1024]{1,0:T(8,128)(2,1)S(1)}) custom-call(bf16[4,256,256]{2,1,0:T(8,128)(2,1)S(1)} %get-tuple-element.36.dft_ref, s32[1,128]{1,0:T(1,128)S(1)} %get-tuple-element.34.seg_ref, f32[4,2,128]{2,1,0:T(2,128)S(1)} %all_to_all.15.stats_ref, f32[128,1024]{1,0:T(8,128)S(1)} %get-tuple-element.46.conv_ref, ...), custom_call_target="tpu_custom_call" | custom-call | flops 671088640 | bytes 3678720 | tf_op jit(solution)/shard_map/filter_grad/pallas_call | solution.py:297
  32.5 26.9 %all_to_all.16.parts_ref = bf16[64,9,2,128]{3,2,1,0:T(2,128)(2,1)S(1)} all-to-all(bf16[64,9,2,128]{3,2,1,0:T(2,128)(2,1)S(1)} %bitcast.6), channel_id=1, replica_groups=mesh['ctx'=64,'x'=4,'z_hi'=2] {'ctx'}, dimensions={0} | all-to-all | bytes 589824 | tf_op jit(solution)/shard_map/all_to_all | solution.py:363
  59.4 1.0 %total.1 = bf16[64,9,2,128]{3,2,1,0:T(2,128)(2,1)} custom-call(bf16[64,9,2,128]{3,2,1,0:T(2,128)(2,1)S(1)} %all_to_all.16.parts_ref), custom_call_target="tpu_custom_call" | custom-call | flops 262144 | bytes 294912 | tf_op jit(solution)/shard_map/total/pallas_call | solution.py:297
  60.5 5.2 %all-to-all-start.2 = ((bf16[64,9,2,128]{3,2,1,0:T(2,128)(2,1)}), bf16[64,9,2,128]{3,2,1,0:T(2,128)(2,1)S(1)}, u32[]{:S(2)}, u32[]{:S(2)}) async-start(bf16[64,9,2,128]{3,2,1,0:T(2,128)(2,1)} %total.1), calls=%async_computation.2 | async-start | bytes 589824 | tf_op jit(solution)/shard_map/all_to_all | solution.py:367
  65.6 2.4 %collective-permute-start.3 = (bf16[128,1024]{1,0:T(8,128)(2,1)S(1)}, bf16[128,1024]{1,0:T(8,128)(2,1)S(1)}, u32[]{:S(2)}, u32[]{:S(2)}) collective-permute-start(bf16[128,1024]{1,0:T(8,128)(2,1)S(1)} %get-tuple-element.54), channel_id=1, source_target_pairs={{8,0},{16,8},{24,16},{32,24},{40,32},{48,40},{56,48},{64,56},{72,6... | collective-permute-start | bytes 786440 | tf_op jit(solution)/shard_map/ppermute | solution.py:368
  68.0 3.2 %out_grads.1 = (bf16[128,1024]{1,0:T(8,128)(2,1)}, bf16[128,1024]{1,0:T(8,128)(2,1)}, f32[128,1024]{1,0:T(8,128)S(1)}, bf16[128,1024]{1,0:T(8,128)(2,1)S(1)}, bf16[128,1024]{1,0:T(8,128)(2,1)S(1)}) custom-call(bf16[128,1024]{1,0:T(8,128)(2,1)} %q_hbm.3, bf16[128,1024]{1,0:T(8,128)(2,1)} %g_hbm.3, bf16[128,1024]{1,0:T(8,128)(2,1)} %k_hbm.5, ...), custom_call_target="tpu_custom_call" | custom-call | flops 805306368 | bytes 3154432 | tf_op jit(solution)/shard_map/out_grads/pallas_call | solution.py:297
  71.2 5.8 %collective-permute-done.3.tail_ref = bf16[128,1024]{1,0:T(8,128)(2,1)S(1)} collective-permute-done((bf16[128,1024]{1,0:T(8,128)(2,1)S(1)}, bf16[128,1024]{1,0:T(8,128)(2,1)S(1)}, u32[]{:S(2)}, u32[]{:S(2)}) %collective-permute-start.3) | collective-permute-done | bytes 262176 | tf_op jit(solution)/shard_map/ppermute | solution.py:368
  77.0 1.6 %input_grads.1 = (bf16[128,1024]{1,0:T(8,128)(2,1)}, bf16[128,1024]{1,0:T(8,128)(2,1)}) custom-call(bf16[4,256,256]{2,1,0:T(8,128)(2,1)S(1)} %get-tuple-element.36.dft_ref, s32[1,128]{1,0:T(1,128)S(1)} %get-tuple-element.34.seg_ref, f32[128,1024]{1,0:T(8,128)S(1)} %get-tuple-element.49.dprod_ref, bf16[128,1024]{1,0:T(8,128)(2,1)S(1)} %collective-permute-done.3.tail_ref, ...), custom_call_target="tpu_custom_call" | custom-call | flops 402653184 | bytes 2884096 | tf_op jit(solution)/shard_map/input_grads/pallas_call | solution.py:297
  78.6 0.2 all-to-all-done.2
  78.9 1.0 %gather.1 = (f32[128,1024]{1,0:T(8,128)}, f32[1,1024]{1,0:T(1,128)}) custom-call(bf16[8,8,9,2,128]{4,3,2,1,0:T(2,128)(2,1)S(1)} %bitcast.5), custom_call_target="tpu_custom_call" | custom-call | flops 262144 | bytes 294912 | tf_op jit(solution)/shard_map/gather/pallas_call | solution.py:297
  (1 shorter events, 0.0 us)
Async XLA Ops:
  0.7 10.0 %collective-permute-start.1 = (bf16[128,1024]{1,0:T(8,128)(2,1)S(1)}, bf16[128,1024]{1,0:T(8,128)(2,1)S(1)}, u32[]{:S(2)}, u32[]{:S(2)}) collective-permute-start(bf16[128,1024]{1,0:T(8,128)(2,1)S(1)} %far_message.1), channel_id=1, source_target_pairs={{56,64},{120,128},{184,192},{248,256},{312,320},{376,384},{440,448... | collective-permute-start | bytes 786440 | tf_op jit(solution)/shard_map/ppermute | solution.py:330
  2.6 9.2 %collective-permute-start = (bf16[128,1024]{1,0:T(8,128)(2,1)S(1)}, bf16[128,1024]{1,0:T(8,128)(2,1)S(1)}, u32[]{:S(2)}, u32[]{:S(2)}) collective-permute-start(bf16[128,1024]{1,0:T(8,128)(2,1)S(1)} %get-tuple-element.37), channel_id=1, source_target_pairs={{0,8},{8,16},{16,24},{24,32},{32,40},{40,48},{48,56},{64,72},{72,8... | collective-permute-start | bytes 786440 | tf_op jit(solution)/shard_map/ppermute | solution.py:331
  12.7 10.2 %collective-permute-start.2 = (f32[4,2,128]{2,1,0:T(2,128)S(1)}, f32[4,2,128]{2,1,0:T(2,128)S(1)}, u32[]{:S(2)}, u32[]{:S(2)}) collective-permute-start(f32[4,2,128]{2,1,0:T(2,128)S(1)} %get-tuple-element.43), channel_id=1, source_target_pairs={{0,1},{1,0},{2,3},{3,2},{4,5},{5,4},{6,7},{7,6},{8,9},{9,8},{10,11... | collective-permute-start | bytes 12296 | tf_op jit(solution)/shard_map/ppermute | solution.py:350
  60.5 18.4 %all-to-all-start.2 = ((bf16[64,9,2,128]{3,2,1,0:T(2,128)(2,1)}), bf16[64,9,2,128]{3,2,1,0:T(2,128)(2,1)S(1)}, u32[]{:S(2)}, u32[]{:S(2)}) async-start(bf16[64,9,2,128]{3,2,1,0:T(2,128)(2,1)} %total.1), calls=%async_computation.2 | async-start | bytes 589824 | tf_op jit(solution)/shard_map/all_to_all | solution.py:367
  65.6 11.4 %collective-permute-start.3 = (bf16[128,1024]{1,0:T(8,128)(2,1)S(1)}, bf16[128,1024]{1,0:T(8,128)(2,1)S(1)}, u32[]{:S(2)}, u32[]{:S(2)}) collective-permute-start(bf16[128,1024]{1,0:T(8,128)(2,1)S(1)} %get-tuple-element.54), channel_id=1, source_target_pairs={{8,0},{16,8},{24,16},{32,24},{40,32},{48,40},{56,48},{64,56},{72,6... | collective-permute-start | bytes 786440 | tf_op jit(solution)/shard_map/ppermute | solution.py:368

commit v6 on v5

--- a/solution.py
+++ b/solution.py
@@ -159,7 +159,7 @@
         copy.wait()
 
 
-def halo_kernel(dft_ref, seg_ref, near_ref, far_ref, taps_ref, own_conv_ref, q_ref, g_ref, gain_ref, conv_ref, stats_ref):
+def halo_kernel(dft_ref, seg_ref, near_ref, far_ref, taps_ref, all_ref, own_conv_ref, q_ref, g_ref, gain_ref, conv_ref, spec_ref, stats_ref):
     seg = seg_ref[...]
     in_first = down(first_doc(seg), BLOCK)
     mark = parity(seg[:, :1])
@@ -169,6 +169,7 @@
         halo = near_ref[:, at] + far_ref[:, at]
         joined = (halo[0:1].astype(jnp.float32) == mark).astype(jnp.float32)
         halo_spec = forward(left, halo) * joined
+        spec_ref[:, at] = all_ref[:, at] + halo_spec
         conv = own_conv_ref[:, at] + in_first * backward(back, times(halo_spec, taps_ref[:, at]))
         conv_ref[:, at] = conv
         y = q_ref[:, at].astype(jnp.float32) * conv
@@ -176,15 +177,6 @@
         inner += lane_sum(g_ref[:, at].astype(jnp.float32) * gain_ref[:, at] * y)
     rows = jnp.concatenate([jnp.sum(square.T, axis=0, keepdims=True), jnp.sum(inner.T, axis=0, keepdims=True)], axis=0)
     stats_ref[...] = jnp.broadcast_to(rows[None], stats_ref.shape)
-
-
-def spectrum_kernel(dft_ref, seg_ref, near_ref, far_ref, all_ref, spec_ref):
-    mark = parity(seg_ref[:, :1])
-    left = dft_ref[2]
-    for at in blocks(all_ref.shape[1]):
-        halo = near_ref[:, at] + far_ref[:, at]
-        joined = (halo[0:1].astype(jnp.float32) == mark).astype(jnp.float32)
-        spec_ref[:, at] = all_ref[:, at] + forward(left, halo) * joined
 
 
 def scales(stats_ref):
@@ -338,17 +330,15 @@
         (seg, prod),
         [pltpu.VMEM(filt.shape, filt.dtype), pltpu.SemaphoreType.DMA((5,))],
     )
-    conv, stats = call(
+    conv, all_spec, stats = call(
         halo_kernel,
         "halo_conv",
-        [wide, ((n_x, 2, ROWS), jnp.float32)],
+        [wide, spec, ((n_x, 2, ROWS), jnp.float32)],
         3 * unit,
         (),
-        (dft, seg, halo, far_halo, taps, own_conv, q_here, g_here, gain_here),
-    )
-    all_spec = call(spectrum_kernel, "spectrum", [spec], unit, (), (dft, seg, halo, far_halo, all_spec))[0]
+        (dft, seg, halo, far_halo, taps, all_spec, own_conv, q_here, g_here, gain_here),
+    )
     stats = stats + lax.ppermute(stats, "z_hi", [(0, 1), (1, 0)])
-    stats, all_spec = lax.optimization_barrier((stats, all_spec))
     stats = lax.all_to_all(stats, "x", 0, 0, tiled=True)
 
     groups = (8, width // ROWS, 9, 2, ROWS)

time: 80.3 us -> 80.3 us (level)
    pallas_call x10 -> x9, Pallas kernels: 13.5 us -> 13.2 us  [call(): pl.pallas_call(kernel, in_specs=[pl.BlockSpec(memory_space=pltpu.HBM)] *...]
where the time goes in v6:
time: 80.3 us; the launch traced here: 79.9 us
  blocking collectives  35.1 us (44%)
  starting transfers between devices  22.8 us (28%)
  Pallas kernels  13.2 us (16%)
  waiting for transfers between devices  8.07 us (10%)
    all_to_all x1, blocking collectives, local(): lax.all_to_all(chunks.reshape(n_ctx, 9, 2, ROWS), 'ctx', 0, 0, tiled=True)  26.9 us
    pallas_call x9, Pallas kernels, call(): pl.pallas_call(kernel, in_specs=[pl.BlockSpec(memory_space=pltpu.HBM)] *...  13.2 us
    ppermute x1, starting transfers between devices, local(): stats = stats + lax.ppermute(stats, 'z_hi', [(0, 1), (1, 0)])  9.25 us
    all_to_all x1, blocking collectives, local(): stats = lax.all_to_all(stats, 'x', 0, 0, tiled=True)  8.15 us
    ppermute x1, waiting for transfers between devices, local(): lax.ppermute(head, 'ctx', [(target, source) for source, target in edges])  5.78 us
    ppermute x1, starting transfers between devices, local(): lax.ppermute(message, 'ctx', [edge for edge in edges if edge[1] % RUN])  5.39 us
    all_to_all x1, starting transfers between devices, local(): full = lax.all_to_all(total, 'ctx', 0, 0, tiled=True)  5.16 us
    ppermute x1, starting transfers between devices, local(): lax.ppermute(head, 'ctx', [(target, source) for source, target in edges])  2.36 us
  transfers between devices with their start and end apart: 5, of which 4 were waited for; matrix products, arithmetic and copies ran while one was open for 0% of the time, Pallas kernels for 11%

profile of v6, /device:TPU:1, one launch (start us, length us, event | category | flops | bytes accessed | tf_op | source)
XLA Modules:
  0.0 79.9 jit_solution(16385825467969146793)
XLA Ops:
  0.6 0.1 far_message.1
  0.7 0.7 collective-permute-start.1
  1.4 1.2 %message.1 = (s32[1,128]{1,0:T(1,128)S(1)}, bf16[128,1024]{1,0:T(8,128)(2,1)S(1)}, bf16[128,1024]{1,0:T(8,128)(2,1)S(1)}) custom-call(s32[1,128]{1,0:T(1,128)} %bitcast.8, bf16[128,1024]{1,0:T(8,128)(2,1)} %k_hbm.5, bf16[128,1024]{1,0:T(8,128)(2,1)} %v_hbm.5), custom_call_target="tpu_custom_call" | custom-call | flops 262144 | bytes 524800 | tf_op jit(solution)/shard_map/message/pallas_call | solution.py:289
  2.6 5.4 %collective-permute-start = (bf16[128,1024]{1,0:T(8,128)(2,1)S(1)}, bf16[128,1024]{1,0:T(8,128)(2,1)S(1)}, u32[]{:S(2)}, u32[]{:S(2)}) collective-permute-start(bf16[128,1024]{1,0:T(8,128)(2,1)S(1)} %get-tuple-element.36), channel_id=1, source_target_pairs={{0,8},{8,16},{16,24},{24,32},{32,40},{40,48},{48,56},{64,72},{72,8... | collective-permute-start | bytes 786440 | tf_op jit(solution)/shard_map/ppermute | solution.py:323
  8.0 2.7 %own_conv.1 = (bf16[4,256,256]{2,1,0:T(8,128)(2,1)S(1)}, bf16[128,1024]{1,0:T(8,128)(2,1)S(1)}, bf16[128,1024]{1,0:T(8,128)(2,1)S(1)}, f32[1,1024]{1,0:T(1,128)S...) custom-call(bf16[4,256,256]{2,1,0:T(8,128)(2,1)} %constant.2.clone.d, ...), custom_call_target="tpu_custom_call" | custom-call | flops 1073741824 | bytes 1839616 | tf_op jit(solution)/shard_map/own_conv/pallas_call | solution.py:289
  10.7 0.0 collective-permute-done.1.far_ref
  10.7 1.1 %collective-permute-done.near_ref = bf16[128,1024]{1,0:T(8,128)(2,1)S(1)} collective-permute-done((bf16[128,1024]{1,0:T(8,128)(2,1)S(1)}, bf16[128,1024]{1,0:T(8,128)(2,1)S(1)}, u32[]{:S(2)}, u32[]{:S(2)}) %collective-permute-start) | collective-permute-done | bytes 262176 | tf_op jit(solution)/shard_map/ppermute | solution.py:323
  11.8 1.0 %halo_conv.1 = (f32[128,1024]{1,0:T(8,128)S(1)}, f32[256,1024]{1,0:T(8,128)S(1)}, f32[4,2,128]{2,1,0:T(2,128)S(1)}) custom-call(bf16[4,256,256]{2,1,0:T(8,128)(2,1)S(1)} %get-tuple-element.35.dft_ref, s32[1,128]{1,0:T(1,128)S(1)} %get-tuple-element.33.seg_ref, bf16[128,1024]{1,0:T(8,128)(2,1)S(1)} %collective-permute-done.near_ref, ...), custom_call_target="tpu_custom_call" | custom-call | flops 402653184 | bytes 4198912 | tf_op jit(solution)/shard_map/halo_conv/pallas_call | solution.py:289
  12.8 9.2 %collective-permute-start.2 = (f32[4,2,128]{2,1,0:T(2,128)S(1)}, f32[4,2,128]{2,1,0:T(2,128)S(1)}, u32[]{:S(2)}, u32[]{:S(2)}) collective-permute-start(f32[4,2,128]{2,1,0:T(2,128)S(1)} %get-tuple-element.43), channel_id=1, source_target_pairs={{0,1},{1,0},{2,3},{3,2},{4,5},{5,4},{6,7},{7,6},{8,9},{9,8},{10,11... | collective-permute-start | bytes 12296 | tf_op jit(solution)/shard_map/ppermute | solution.py:341
  22.0 1.0 %collective-permute-done.2 = f32[4,2,128]{2,1,0:T(2,128)S(1)} collective-permute-done((f32[4,2,128]{2,1,0:T(2,128)S(1)}, f32[4,2,128]{2,1,0:T(2,128)S(1)}, u32[]{:S(2)}, u32[]{:S(2)}) %collective-permute-start.2) | collective-permute-done | bytes 4128 | tf_op jit(solution)/shard_map/ppermute | solution.py:341
  23.0 8.1 %all_to_all.15.stats_ref = f32[4,2,128]{2,1,0:T(2,128)S(1)} all-to-all(f32[4,2,128]{2,1,0:T(2,128)S(1)} %add.3), channel_id=1, replica_groups=mesh['ctx'=64,'x'=4,'z_hi'=2] {'x'}, dimensions={0} | all-to-all | bytes 8192 | tf_op jit(solution)/shard_map/all_to_all | solution.py:342
  31.2 1.4 %filter_grad.1 = (bf16[8,8,9,2,128]{4,3,2,1,0:T(2,128)(2,1)S(1)}, bf16[128,1024]{1,0:T(8,128)(2,1)S(1)}) custom-call(bf16[4,256,256]{2,1,0:T(8,128)(2,1)S(1)} %get-tuple-element.35.dft_ref, s32[1,128]{1,0:T(1,128)S(1)} %get-tuple-element.33.seg_ref, f32[4,2,128]{2,1,0:T(2,128)S(1)} %all_to_all.15.stats_ref, f32[128,1024]{1,0:T(8,128)S(1)} %get-tuple-element.44.conv_ref, ...), custom_call_target="tpu_custom_call" | custom-call | flops 671088640 | bytes 3678720 | tf_op jit(solution)/shard_map/filter_grad/pallas_call | solution.py:289
  32.6 26.9 %all_to_all.16.parts_ref = bf16[64,9,2,128]{3,2,1,0:T(2,128)(2,1)S(1)} all-to-all(bf16[64,9,2,128]{3,2,1,0:T(2,128)(2,1)S(1)} %bitcast.6), channel_id=1, replica_groups=mesh['ctx'=64,'x'=4,'z_hi'=2] {'ctx'}, dimensions={0} | all-to-all | bytes 589824 | tf_op jit(solution)/shard_map/all_to_all | solution.py:353
  59.5 1.0 %total.1 = bf16[64,9,2,128]{3,2,1,0:T(2,128)(2,1)} custom-call(bf16[64,9,2,128]{3,2,1,0:T(2,128)(2,1)S(1)} %all_to_all.16.parts_ref), custom_call_target="tpu_custom_call" | custom-call | flops 262144 | bytes 294912 | tf_op jit(solution)/shard_map/total/pallas_call | solution.py:289
  60.5 5.2 %all-to-all-start.2 = ((bf16[64,9,2,128]{3,2,1,0:T(2,128)(2,1)}), bf16[64,9,2,128]{3,2,1,0:T(2,128)(2,1)S(1)}, u32[]{:S(2)}, u32[]{:S(2)}) async-start(bf16[64,9,2,128]{3,2,1,0:T(2,128)(2,1)} %total.1), calls=%async_computation.2 | async-start | bytes 589824 | tf_op jit(solution)/shard_map/all_to_all | solution.py:357
  65.7 2.4 %collective-permute-start.3 = (bf16[128,1024]{1,0:T(8,128)(2,1)S(1)}, bf16[128,1024]{1,0:T(8,128)(2,1)S(1)}, u32[]{:S(2)}, u32[]{:S(2)}) collective-permute-start(bf16[128,1024]{1,0:T(8,128)(2,1)S(1)} %get-tuple-element.52), channel_id=1, source_target_pairs={{8,0},{16,8},{24,16},{32,24},{40,32},{48,40},{56,48},{64,56},{72,6... | collective-permute-start | bytes 786440 | tf_op jit(solution)/shard_map/ppermute | solution.py:358
  68.0 3.2 %out_grads.1 = (bf16[128,1024]{1,0:T(8,128)(2,1)}, bf16[128,1024]{1,0:T(8,128)(2,1)}, f32[128,1024]{1,0:T(8,128)S(1)}, bf16[128,1024]{1,0:T(8,128)(2,1)S(1)}, bf16[128,1024]{1,0:T(8,128)(2,1)S(1)}) custom-call(bf16[128,1024]{1,0:T(8,128)(2,1)} %q_hbm.3, bf16[128,1024]{1,0:T(8,128)(2,1)} %g_hbm.3, bf16[128,1024]{1,0:T(8,128)(2,1)} %k_hbm.5, ...), custom_call_target="tpu_custom_call" | custom-call | flops 805306368 | bytes 3154432 | tf_op jit(solution)/shard_map/out_grads/pallas_call | solution.py:289
  71.3 5.8 %collective-permute-done.3.tail_ref = bf16[128,1024]{1,0:T(8,128)(2,1)S(1)} collective-permute-done((bf16[128,1024]{1,0:T(8,128)(2,1)S(1)}, bf16[128,1024]{1,0:T(8,128)(2,1)S(1)}, u32[]{:S(2)}, u32[]{:S(2)}) %collective-permute-start.3) | collective-permute-done | bytes 262176 | tf_op jit(solution)/shard_map/ppermute | solution.py:358
  77.0 1.6 %input_grads.1 = (bf16[128,1024]{1,0:T(8,128)(2,1)}, bf16[128,1024]{1,0:T(8,128)(2,1)}) custom-call(bf16[4,256,256]{2,1,0:T(8,128)(2,1)S(1)} %get-tuple-element.35.dft_ref, s32[1,128]{1,0:T(1,128)S(1)} %get-tuple-element.33.seg_ref, f32[128,1024]{1,0:T(8,128)S(1)} %get-tuple-element.47.dprod_ref, bf16[128,1024]{1,0:T(8,128)(2,1)S(1)} %collective-permute-done.3.tail_ref, ...), custom_call_target="tpu_custom_call" | custom-call | flops 402653184 | bytes 2884096 | tf_op jit(solution)/shard_map/input_grads/pallas_call | solution.py:289
  78.7 0.2 all-to-all-done.2
  78.9 1.0 %gather.1 = (f32[128,1024]{1,0:T(8,128)}, f32[1,1024]{1,0:T(1,128)}) custom-call(bf16[8,8,9,2,128]{4,3,2,1,0:T(2,128)(2,1)S(1)} %bitcast.5), custom_call_target="tpu_custom_call" | custom-call | flops 262144 | bytes 294912 | tf_op jit(solution)/shard_map/gather/pallas_call | solution.py:289
  (1 shorter events, 0.0 us)
Async XLA Ops:
  0.7 10.0 %collective-permute-start.1 = (bf16[128,1024]{1,0:T(8,128)(2,1)S(1)}, bf16[128,1024]{1,0:T(8,128)(2,1)S(1)}, u32[]{:S(2)}, u32[]{:S(2)}) collective-permute-start(bf16[128,1024]{1,0:T(8,128)(2,1)S(1)} %far_message.1), channel_id=1, source_target_pairs={{56,64},{120,128},{184,192},{248,256},{312,320},{376,384},{440,448... | collective-permute-start | bytes 786440 | tf_op jit(solution)/shard_map/ppermute | solution.py:322
  2.6 9.2 %collective-permute-start = (bf16[128,1024]{1,0:T(8,128)(2,1)S(1)}, bf16[128,1024]{1,0:T(8,128)(2,1)S(1)}, u32[]{:S(2)}, u32[]{:S(2)}) collective-permute-start(bf16[128,1024]{1,0:T(8,128)(2,1)S(1)} %get-tuple-element.36), channel_id=1, source_target_pairs={{0,8},{8,16},{16,24},{24,32},{32,40},{40,48},{48,56},{64,72},{72,8... | collective-permute-start | bytes 786440 | tf_op jit(solution)/shard_map/ppermute | solution.py:323
  12.8 10.2 %collective-permute-start.2 = (f32[4,2,128]{2,1,0:T(2,128)S(1)}, f32[4,2,128]{2,1,0:T(2,128)S(1)}, u32[]{:S(2)}, u32[]{:S(2)}) collective-permute-start(f32[4,2,128]{2,1,0:T(2,128)S(1)} %get-tuple-element.43), channel_id=1, source_target_pairs={{0,1},{1,0},{2,3},{3,2},{4,5},{5,4},{6,7},{7,6},{8,9},{9,8},{10,11... | collective-permute-start | bytes 12296 | tf_op jit(solution)/shard_map/ppermute | solution.py:341
  60.5 18.4 %all-to-all-start.2 = ((bf16[64,9,2,128]{3,2,1,0:T(2,128)(2,1)}), bf16[64,9,2,128]{3,2,1,0:T(2,128)(2,1)S(1)}, u32[]{:S(2)}, u32[]{:S(2)}) async-start(bf16[64,9,2,128]{3,2,1,0:T(2,128)(2,1)} %total.1), calls=%async_computation.2 | async-start | bytes 589824 | tf_op jit(solution)/shard_map/all_to_all | solution.py:357
  65.7 11.4 %collective-permute-start.3 = (bf16[128,1024]{1,0:T(8,128)(2,1)S(1)}, bf16[128,1024]{1,0:T(8,128)(2,1)S(1)}, u32[]{:S(2)}, u32[]{:S(2)}) collective-permute-start(bf16[128,1024]{1,0:T(8,128)(2,1)S(1)} %get-tuple-element.52), channel_id=1, source_target_pairs={{8,0},{16,8},{24,16},{32,24},{40,32},{48,40},{56,48},{64,56},{72,6... | collective-permute-start | bytes 786440 | tf_op jit(solution)/shard_map/ppermute | solution.py:358
